TPU v7x, 256 devices: a whole 4x4x8 slice. The times are simulated.
256 devices in a mesh: cluster: 8 (over y, core), sub: 32 (over x, z).
Axes of the slice: x: 4, y: 4, z: 8, core: 2. Of those that a mesh axis runs over, the one named last changes fastest.
Arguments:
- compliance: float32 [8, 32, 1024, 1024], P('cluster', 'sub'), may hold values from -0.078125 to 4.078125, as said below
- loads: float32 [8, 32, 1024, 256], P('cluster', 'sub'), may hold values from -6 to 6
- modes: float32 [8, 32, 32, 1024], P('cluster', 'sub'), may hold values from -1 to 1
- coarse_inverse: float32 [8, 1024, 1024], P('cluster', 'sub'), may hold values from -0.9 to 0.9, as said below
- face_block: int32 [8, 32, 4], replicated, may hold values from 0 to 7, as said below
- edge_rows: int32 [8, 32, 2], replicated, may hold values from 16 to 128
Outputs:
- solution: float32 [8, 32, 1024, 256], P('cluster', 'sub')
- residual: float32 [8, 32, 1024, 256], P('cluster', 'sub')
Inputs may be any that keep to these rules, and one draw needn't show every extreme that they name: `compliance`: symmetric positive definite for every subdomain. `coarse_inverse`: symmetric positive definite for every cluster. `face_block`: the four faces of a subdomain lie in four different row blocks. `edge_rows`: entries of faces with no partner are not read.
All inputs are finite; a program needn't handle non-finite values.
Results may differ from a plain program's by a relative error of at most 0.00018.
Values sent between devices are 32-bit elements; how exact they have to be, the bound alone decides.
A program may use at most 64 MiB of HBM per device.

v0:
```python
import jax
import jax.numpy as jnp
from jax import lax
from jax.sharding import Mesh
from jax.sharding import PartitionSpec as P

BLOCK = 128
ITERS = 3
SUB = ("sub_0", "sub_1")
CLUSTER = ("cluster_0", "cluster_1")
CLUSTER_SUB = ("cluster_0", "cluster_1", "sub_0", "sub_1")


def from_behind(value, axis, steps):
    count = lax.axis_size(axis)
    initial, last = (max(0, -steps), min(count, count - steps))
    return lax.ppermute(value, axis, [(source, source + steps) for source in range(initial, last)])


def copy_for_each(x, axis):
    copies = jnp.broadcast_to(x, (lax.axis_size(axis), *x.shape))
    return lax.all_to_all(copies, axis, split_axis=0, concat_axis=0, tiled=True)


def in_order(parts, dim):
    shape = list(parts.shape[1:])
    shape[dim] *= parts.shape[0]
    return jnp.moveaxis(parts, 0, dim).reshape(shape)


def collect(x, axis, dim):
    parts = copy_for_each(x, axis)
    return in_order(parts, dim)


def one_axis_at_a_time(x, axes):
    for axis in axes:
        x = lax.psum(x, axis)
    return x


def take_block(field, block_index):
    return lax.dynamic_slice_in_dim(field, block_index * BLOCK, BLOCK, 0)


def add_block(field, block_index, arrived, length):
    rows = jnp.arange(BLOCK, dtype=jnp.int32)
    weight = (0.5 * (rows < length).astype(jnp.float32))[:, None]
    current = take_block(field, block_index)
    return lax.dynamic_update_slice_in_dim(
        field, current + weight * arrived, block_index * BLOCK, 0
    )


def assemble(field, faces, sub_routes, clus_routes):
    result = field
    for send_face, recv_face, length, offset in sub_routes:
        arrived = from_behind(take_block(field, faces[send_face]), SUB, offset)
        result = add_block(result, faces[recv_face], arrived, length)
    for send_face, recv_face, length, offset in clus_routes:
        arrived = from_behind(take_block(field, faces[send_face]), CLUSTER, offset)
        result = add_block(result, faces[recv_face], arrived, length)
    return result


def precondition(basis, inverse_rows, resid):
    coarse = jnp.dot(basis, resid, precision=lax.Precision.HIGHEST)
    solved = jnp.dot(inverse_rows, collect(coarse, SUB, 0), precision=lax.Precision.HIGHEST)
    return resid + jnp.einsum("mo,ml->ol", basis, solved, precision=lax.Precision.HIGHEST)


def paired_dots(first, second, third):
    return (
        one_axis_at_a_time(jnp.sum(first * second, axis=0), CLUSTER_SUB),
        one_axis_at_a_time(jnp.sum(third * second, axis=0), CLUSTER_SUB),
    )


def shards(compliance, loads, modes, coarse_inverse, face_block, edge_rows):
    matrix = compliance[0, 0]
    rhs = loads[0, 0]
    basis = modes[0, 0]
    inverse_rows = coarse_inverse[0]
    clus_index = lax.axis_index(CLUSTER)
    sub_index = lax.axis_index(SUB)
    faces = face_block[clus_index, sub_index]
    sub_low = edge_rows[clus_index, jnp.maximum(sub_index - 1, 0), 0]
    sub_high = edge_rows[clus_index, sub_index, 0]
    clus_low = edge_rows[jnp.maximum(clus_index - 1, 0), sub_index, 1]
    clus_high = edge_rows[clus_index, sub_index, 1]
    sub_routes = ((1, 0, sub_low, 1), (0, 1, sub_high, -1))
    clus_routes = ((3, 2, clus_low, 1), (2, 3, clus_high, -1))

    def operator(field):
        inner = assemble(field, faces, sub_routes, clus_routes)
        product = jnp.dot(matrix, inner, precision=lax.Precision.HIGHEST)
        return assemble(product, faces, sub_routes, clus_routes)

    solution = jnp.zeros_like(rhs)
    residual = rhs
    precond = precondition(basis, inverse_rows, residual)
    image = operator(precond)
    rz_now, curve = paired_dots(residual, precond, image)
    alpha = rz_now / curve
    direction, along = (precond, image)
    for step in range(ITERS):
        solution = solution + alpha * direction
        residual = residual - alpha * along
        if step + 1 < ITERS:
            precond = precondition(basis, inverse_rows, residual)
            image = operator(precond)
            rz_next, curve = paired_dots(residual, precond, image)
            ratio = rz_next / rz_now
            alpha = rz_next / (curve - ratio * rz_next / alpha)
            direction = precond + ratio * direction
            along = image + ratio * along
            rz_now = rz_next
    return (solution[None, None], residual[None, None])


def solution(mesh):
    finer = Mesh(mesh.devices.reshape(4, 2, 4, 8), ("cluster_0", "cluster_1", "sub_0", "sub_1"))
    in_specs = (
        P(CLUSTER, SUB, None, None),
        P(CLUSTER, SUB, None, None),
        P(CLUSTER, SUB, None, None),
        P(CLUSTER, SUB, None),
        P(),
        P(),
    )
    out_specs = (P(CLUSTER, SUB, None, None), P(CLUSTER, SUB, None, None))
    return jax.shard_map(
        shards, mesh=finer, in_specs=in_specs, out_specs=out_specs, check_vma=False
    )
```

profile of v0, /device:TPU:1, one launch (start us, length us, event | category | flops | bytes accessed | tf_op | source)
XLA Modules:
  0.0 351.5 jit_solution(10099001294566867141)
XLA Ops:
  4.4 11.9 %all-to-all-start = ((f32[32,32,256]{2,1,0:T(8,128)}), f32[32,32,256]{2,1,0:T(8,128)S(1)}, u32[]{:S(2)}, u32[]{:S(2)}) async-start(f32[32,32,256]{2,1,0:T(8,128)} %broadcast_in_dim.10), calls=%async_computation | async-start | bytes 2097152 | tf_op jit(solution)/shard_map/all_to_all | solution.py:22
  20.2 20.8 %all-to-all-done = f32[32,32,256]{2,1,0:T(8,128)S(1)} async-done(((f32[32,32,256]{2,1,0:T(8,128)}), f32[32,32,256]{2,1,0:T(8,128)S(1)}, u32[]{:S(2)}, u32[]{:S(2)}) %all-to-all-start) | async-done | bytes 1048608 | tf_op jit(solution)/shard_map/all_to_all | solution.py:22
  43.8 6.1 %collective-permute-start = (f32[128,256]{0,1:T(8,128)S(1)}, f32[128,256]{0,1:T(8,128)}, u32[]{:S(2)}, u32[]{:S(2)}) collective-permute-start(f32[128,256]{0,1:T(8,128)S(1)} %constant_dynamic-slice_fusion.11), channel_id=1, source_target_pairs={{0,1},{1,2},{2,3},{3,4},{4,5},{5,6},{6,7},{7,8},{8,9},{9,10},{10,1... | collective-permute-start | bytes 393224 | tf_op jit(solution)/shard_map/ppermute | solution.py:17
  57.0 5.0 %collective-permute-start.3 = (f32[128,256]{0,1:T(8,128)S(1)}, f32[128,256]{0,1:T(8,128)S(1)}, u32[]{:S(2)}, u32[]{:S(2)}) collective-permute-start(f32[128,256]{0,1:T(8,128)S(1)} %get-tuple-element.59), channel_id=1, source_target_pairs={{32,0},{64,32},{96,64},{128,96},{160,128},{192,160},{224,192},{33,... | collective-permute-start | bytes 393224 | tf_op jit(solution)/shard_map/ppermute | solution.py:17
  88.1 8.5 %all-reduce.8 = (f32[256]{0:T(256)S(1)}, f32[256]{0:T(256)S(1)}) all-reduce(f32[256]{0:T(256)S(1)} %get-tuple-element.9, f32[256]{0:T(256)S(1)} %get-tuple-element.8), channel_id=1, replica_groups=mesh['cluster_0'=4,'cluster_1'=2,'sub_0'=4,'sub_1'=8] {'cluster_0'}, use_global_device_ids=true, to_apply=%region_1.0 | all-reduce | flops 512 | bytes 4096 | tf_op jit(solution)/shard_map/psum | solution.py:38
  96.6 4.8 %all-reduce.11 = (f32[256]{0:T(256)S(1)}, f32[256]{0:T(256)S(1)}) all-reduce(f32[256]{0:T(256)S(1)} %get-tuple-element.26, f32[256]{0:T(256)S(1)} %get-tuple-element.27), channel_id=1, replica_groups=mesh['cluster_0'=4,'cluster_1'=2,'sub_0'=4,'sub_1'=8] {'cluster_1'}, use_global_device_ids=true, to_apply=%region_2.0 | all-reduce | flops 512 | bytes 4096 | tf_op jit(solution)/shard_map/psum | solution.py:38
  101.4 8.0 %all-reduce.5 = (f32[256]{0:T(256)S(1)}, f32[256]{0:T(256)S(1)}) all-reduce(f32[256]{0:T(256)S(1)} %get-tuple-element.32, f32[256]{0:T(256)S(1)} %get-tuple-element.33), channel_id=1, replica_groups=mesh['cluster_0'=4,'cluster_1'=2,'sub_0'=4,'sub_1'=8] {'sub_0'}, use_global_device_ids=true, to_apply=%region_3.0 | all-reduce | flops 512 | bytes 4096 | tf_op jit(solution)/shard_map/psum | solution.py:38
  109.4 13.6 %all-reduce.2 = (f32[256]{0:T(256)S(1)}, f32[256]{0:T(256)S(1)}) all-reduce(f32[256]{0:T(256)S(1)} %get-tuple-element.20, f32[256]{0:T(256)S(1)} %get-tuple-element.21), channel_id=1, replica_groups=mesh['cluster_0'=4,'cluster_1'=2,'sub_0'=4,'sub_1'=8] {'sub_1'}, use_global_device_ids=true, to_apply=%region_4.0 | all-reduce | flops 512 | bytes 4096 | tf_op jit(solution)/shard_map/psum | solution.py:38
  125.5 23.5 %all_to_all.15 = f32[32,32,256]{2,1,0:T(8,128)S(1)} all-to-all(f32[32,32,256]{2,1,0:T(8,128)S(1)} %broadcast_in_dim.11), channel_id=1, replica_groups=mesh['cluster_0'=4,'cluster_1'=2,'sub_0'=4,'sub_1'=8] {'sub_0','sub_1'}, dimensions={0} | all-to-all | bytes 2097152 | tf_op jit(solution)/shard_map/all_to_all | solution.py:22
  151.8 5.4 %collective-permute-start.8 = (f32[128,256]{0,1:T(8,128)S(1)}, f32[128,256]{0,1:T(8,128)S(1)}, u32[]{:S(2)}, u32[]{:S(2)}) collective-permute-start(f32[128,256]{0,1:T(8,128)S(1)} %constant_dynamic-slice_fusion.4), channel_id=1, source_target_pairs={{0,1},{1,2},{2,3},{3,4},{4,5},{5,6},{6,7},{7,8},{8,9},{9,10},{10,1... | collective-permute-start | bytes 393224 | tf_op jit(solution)/shard_map/ppermute | solution.py:17
  160.6 10.6 %collective-permute-start.11 = (f32[128,256]{0,1:T(8,128)S(1)}, f32[128,256]{0,1:T(8,128)S(1)}, u32[]{:S(2)}, u32[]{:S(2)}) collective-permute-start(f32[128,256]{0,1:T(8,128)S(1)} %get-tuple-element.51), channel_id=1, source_target_pairs={{32,0},{64,32},{96,64},{128,96},{160,128},{192,160},{224,192},{33,... | collective-permute-start | bytes 393224 | tf_op jit(solution)/shard_map/ppermute | solution.py:17
  179.4 4.7 %collective-permute-start.12 = (f32[128,256]{0,1:T(8,128)S(1)}, f32[128,256]{0,1:T(8,128)S(1)}, u32[]{:S(2)}, u32[]{:S(2)}) collective-permute-start(f32[128,256]{0,1:T(8,128)S(1)} %get-tuple-element.49), channel_id=1, source_target_pairs={{0,1},{1,2},{2,3},{3,4},{4,5},{5,6},{6,7},{7,8},{8,9},{9,10},{10,1... | collective-permute-start | bytes 393224 | tf_op jit(solution)/shard_map/ppermute | solution.py:17
  198.2 7.2 %all-reduce.7 = (f32[256]{0:T(256)S(1)}, f32[256]{0:T(256)S(1)}) all-reduce(f32[256]{0:T(256)S(1)} %get-tuple-element.7, f32[256]{0:T(256)S(1)} %get-tuple-element.6), channel_id=1, replica_groups=mesh['cluster_0'=4,'cluster_1'=2,'sub_0'=4,'sub_1'=8] {'cluster_0'}, use_global_device_ids=true, to_apply=%region_11.0 | all-reduce | flops 512 | bytes 4096 | tf_op jit(solution)/shard_map/psum | solution.py:38
  205.4 5.2 %all-reduce.10 = (f32[256]{0:T(256)S(1)}, f32[256]{0:T(256)S(1)}) all-reduce(f32[256]{0:T(256)S(1)} %get-tuple-element.24, f32[256]{0:T(256)S(1)} %get-tuple-element.25), channel_id=1, replica_groups=mesh['cluster_0'=4,'cluster_1'=2,'sub_0'=4,'sub_1'=8] {'cluster_1'}, use_global_device_ids=true, to_apply=%region_12.0 | all-reduce | flops 512 | bytes 4096 | tf_op jit(solution)/shard_map/psum | solution.py:38
  210.6 8.6 %all-reduce.4 = (f32[256]{0:T(256)S(1)}, f32[256]{0:T(256)S(1)}) all-reduce(f32[256]{0:T(256)S(1)} %get-tuple-element.30, f32[256]{0:T(256)S(1)} %get-tuple-element.31), channel_id=1, replica_groups=mesh['cluster_0'=4,'cluster_1'=2,'sub_0'=4,'sub_1'=8] {'sub_0'}, use_global_device_ids=true, to_apply=%region_13.0 | all-reduce | flops 512 | bytes 4096 | tf_op jit(solution)/shard_map/psum | solution.py:38
  219.2 13.6 %all-reduce.1 = (f32[256]{0:T(256)S(1)}, f32[256]{0:T(256)S(1)}) all-reduce(f32[256]{0:T(256)S(1)} %get-tuple-element.18, f32[256]{0:T(256)S(1)} %get-tuple-element.19), channel_id=1, replica_groups=mesh['cluster_0'=4,'cluster_1'=2,'sub_0'=4,'sub_1'=8] {'sub_1'}, use_global_device_ids=true, to_apply=%region_14.0 | all-reduce | flops 512 | bytes 4096 | tf_op jit(solution)/shard_map/psum | solution.py:38
  235.5 23.7 %all_to_all.16 = f32[32,32,256]{2,1,0:T(8,128)S(1)} all-to-all(f32[32,32,256]{2,1,0:T(8,128)S(1)} %broadcast_in_dim.12), channel_id=1, replica_groups=mesh['cluster_0'=4,'cluster_1'=2,'sub_0'=4,'sub_1'=8] {'sub_0','sub_1'}, dimensions={0} | all-to-all | bytes 2097152 | tf_op jit(solution)/shard_map/all_to_all | solution.py:22
  262.0 5.4 %collective-permute-start.16 = (f32[128,256]{0,1:T(8,128)S(1)}, f32[128,256]{0,1:T(8,128)S(1)}, u32[]{:S(2)}, u32[]{:S(2)}) collective-permute-start(f32[128,256]{0,1:T(8,128)S(1)} %constant_dynamic-slice_fusion), channel_id=1, source_target_pairs={{0,1},{1,2},{2,3},{3,4},{4,5},{5,6},{6,7},{7,8},{8,9},{9,10},{10,1... | collective-permute-start | bytes 393224 | tf_op jit(solution)/shard_map/ppermute | solution.py:17
  270.7 10.6 %collective-permute-start.19 = (f32[128,256]{0,1:T(8,128)S(1)}, f32[128,256]{0,1:T(8,128)S(1)}, u32[]{:S(2)}, u32[]{:S(2)}) collective-permute-start(f32[128,256]{0,1:T(8,128)S(1)} %get-tuple-element.43), channel_id=1, source_target_pairs={{32,0},{64,32},{96,64},{128,96},{160,128},{192,160},{224,192},{33,... | collective-permute-start | bytes 393224 | tf_op jit(solution)/shard_map/ppermute | solution.py:17
  289.1 4.8 %collective-permute-start.20 = (f32[128,256]{0,1:T(8,128)S(1)}, f32[128,256]{0,1:T(8,128)S(1)}, u32[]{:S(2)}, u32[]{:S(2)}) collective-permute-start(f32[128,256]{0,1:T(8,128)S(1)} %get-tuple-element.41), channel_id=1, source_target_pairs={{0,1},{1,2},{2,3},{3,4},{4,5},{5,6},{6,7},{7,8},{8,9},{9,10},{10,1... | collective-permute-start | bytes 393224 | tf_op jit(solution)/shard_map/ppermute | solution.py:17
  307.7 7.2 %all-reduce.6 = (f32[256]{0:T(256)S(1)}, f32[256]{0:T(256)S(1)}) all-reduce(f32[256]{0:T(256)S(1)} %get-tuple-element.5, f32[256]{0:T(256)S(1)} %get-tuple-element.4), channel_id=1, replica_groups=mesh['cluster_0'=4,'cluster_1'=2,'sub_0'=4,'sub_1'=8] {'cluster_0'}, use_global_device_ids=true, to_apply=%region_21.0 | all-reduce | flops 512 | bytes 4096 | tf_op jit(solution)/shard_map/psum | solution.py:38
  314.8 5.2 %all-reduce.9 = (f32[256]{0:T(256)S(1)}, f32[256]{0:T(256)S(1)}) all-reduce(f32[256]{0:T(256)S(1)} %get-tuple-element.22, f32[256]{0:T(256)S(1)} %get-tuple-element.23), channel_id=1, replica_groups=mesh['cluster_0'=4,'cluster_1'=2,'sub_0'=4,'sub_1'=8] {'cluster_1'}, use_global_device_ids=true, to_apply=%region_22.0 | all-reduce | flops 512 | bytes 4096 | tf_op jit(solution)/shard_map/psum | solution.py:38
  320.0 8.7 %all-reduce.3 = (f32[256]{0:T(256)S(1)}, f32[256]{0:T(256)S(1)}) all-reduce(f32[256]{0:T(256)S(1)} %get-tuple-element.28, f32[256]{0:T(256)S(1)} %get-tuple-element.29), channel_id=1, replica_groups=mesh['cluster_0'=4,'cluster_1'=2,'sub_0'=4,'sub_1'=8] {'sub_0'}, use_global_device_ids=true, to_apply=%region_23.0 | all-reduce | flops 512 | bytes 4096 | tf_op jit(solution)/shard_map/psum | solution.py:38
  328.6 13.6 %all-reduce = (f32[256]{0:T(256)S(1)}, f32[256]{0:T(256)S(1)}) all-reduce(f32[256]{0:T(256)S(1)} %get-tuple-element.16, f32[256]{0:T(256)S(1)} %get-tuple-element.17), channel_id=1, replica_groups=mesh['cluster_0'=4,'cluster_1'=2,'sub_0'=4,'sub_1'=8] {'sub_1'}, use_global_device_ids=true, to_apply=%region_24.0 | all-reduce | flops 512 | bytes 4096 | tf_op jit(solution)/shard_map/psum | solution.py:38
  (136 shorter events, 110.9 us)
Async XLA Ops:
  4.4 36.5 %all-to-all-start = ((f32[32,32,256]{2,1,0:T(8,128)}), f32[32,32,256]{2,1,0:T(8,128)S(1)}, u32[]{:S(2)}, u32[]{:S(2)}) async-start(f32[32,32,256]{2,1,0:T(8,128)} %broadcast_in_dim.10), calls=%async_computation | async-start | bytes 2097152 | tf_op jit(solution)/shard_map/all_to_all | solution.py:22
  43.8 9.4 %collective-permute-start = (f32[128,256]{0,1:T(8,128)S(1)}, f32[128,256]{0,1:T(8,128)}, u32[]{:S(2)}, u32[]{:S(2)}) collective-permute-start(f32[128,256]{0,1:T(8,128)S(1)} %constant_dynamic-slice_fusion.11), channel_id=1, source_target_pairs={{0,1},{1,2},{2,3},{3,4},{4,5},{5,6},{6,7},{7,8},{8,9},{9,10},{10,1... | collective-permute-start | bytes 393224 | tf_op jit(solution)/shard_map/ppermute | solution.py:17
  54.4 10.8 %collective-permute-start.1 = (f32[128,256]{0,1:T(8,128)S(1)}, f32[128,256]{0,1:T(8,128)S(1)}, u32[]{:S(2)}, u32[]{:S(2)}) collective-permute-start(f32[128,256]{0,1:T(8,128)S(1)} %get-tuple-element.62), channel_id=1, source_target_pairs={{1,0},{2,1},{3,2},{4,3},{5,4},{6,5},{7,6},{8,7},{9,8},{10,9},{11,1... | collective-permute-start | bytes 393224 | tf_op jit(solution)/shard_map/ppermute | solution.py:17
  57.0 10.1 %collective-permute-start.3 = (f32[128,256]{0,1:T(8,128)S(1)}, f32[128,256]{0,1:T(8,128)S(1)}, u32[]{:S(2)}, u32[]{:S(2)}) collective-permute-start(f32[128,256]{0,1:T(8,128)S(1)} %get-tuple-element.59), channel_id=1, source_target_pairs={{32,0},{64,32},{96,64},{128,96},{160,128},{192,160},{224,192},{33,... | collective-permute-start | bytes 393224 | tf_op jit(solution)/shard_map/ppermute | solution.py:17
  62.0 5.0 %collective-permute-start.2 = (f32[128,256]{0,1:T(8,128)S(1)}, f32[128,256]{0,1:T(8,128)S(1)}, u32[]{:S(2)}, u32[]{:S(2)}) collective-permute-start(f32[128,256]{0,1:T(8,128)S(1)} %get-tuple-element.60), channel_id=1, source_target_pairs={{0,32},{32,64},{64,96},{96,128},{128,160},{160,192},{192,224},{1,3... | collective-permute-start | bytes 393224 | tf_op jit(solution)/shard_map/ppermute | solution.py:17
  71.0 12.2 %collective-permute-start.4 = (f32[128,256]{0,1:T(8,128)S(1)}, f32[128,256]{0,1:T(8,128)S(1)}, u32[]{:S(2)}, u32[]{:S(2)}) collective-permute-start(f32[128,256]{0,1:T(8,128)S(1)} %get-tuple-element.57), channel_id=1, source_target_pairs={{0,1},{1,2},{2,3},{3,4},{4,5},{5,6},{6,7},{7,8},{8,9},{9,10},{10,1... | collective-permute-start | bytes 393224 | tf_op jit(solution)/shard_map/ppermute | solution.py:17
  75.3 12.4 %collective-permute-start.7 = (f32[128,256]{0,1:T(8,128)S(1)}, f32[128,256]{0,1:T(8,128)S(1)}, u32[]{:S(2)}, u32[]{:S(2)}) collective-permute-start(f32[128,256]{0,1:T(8,128)S(1)} %get-tuple-element.55), channel_id=1, source_target_pairs={{32,0},{64,32},{96,64},{128,96},{160,128},{192,160},{224,192},{33,... | collective-permute-start | bytes 393224 | tf_op jit(solution)/shard_map/ppermute | solution.py:17
  77.2 10.4 %collective-permute-start.6 = (f32[128,256]{0,1:T(8,128)S(1)}, f32[128,256]{0,1:T(8,128)S(1)}, u32[]{:S(2)}, u32[]{:S(2)}) collective-permute-start(f32[128,256]{0,1:T(8,128)S(1)} %get-tuple-element.56), channel_id=1, source_target_pairs={{0,32},{32,64},{64,96},{96,128},{128,160},{160,192},{192,224},{1,3... | collective-permute-start | bytes 393224 | tf_op jit(solution)/shard_map/ppermute | solution.py:17
  81.9 5.7 %collective-permute-start.5 = (f32[128,256]{0,1:T(8,128)S(1)}, f32[128,256]{0,1:T(8,128)S(1)}, u32[]{:S(2)}, u32[]{:S(2)}) collective-permute-start(f32[128,256]{0,1:T(8,128)S(1)} %get-tuple-element.58), channel_id=1, source_target_pairs={{1,0},{2,1},{3,2},{4,3},{5,4},{6,5},{7,6},{8,7},{9,8},{10,9},{11,1... | collective-permute-start | bytes 393224 | tf_op jit(solution)/shard_map/ppermute | solution.py:17
  151.8 7.4 %collective-permute-start.8 = (f32[128,256]{0,1:T(8,128)S(1)}, f32[128,256]{0,1:T(8,128)S(1)}, u32[]{:S(2)}, u32[]{:S(2)}) collective-permute-start(f32[128,256]{0,1:T(8,128)S(1)} %constant_dynamic-slice_fusion.4), channel_id=1, source_target_pairs={{0,1},{1,2},{2,3},{3,4},{4,5},{5,6},{6,7},{7,8},{8,9},{9,10},{10,1... | collective-permute-start | bytes 393224 | tf_op jit(solution)/shard_map/ppermute | solution.py:17
  159.3 14.3 %collective-permute-start.9 = (f32[128,256]{0,1:T(8,128)S(1)}, f32[128,256]{0,1:T(8,128)S(1)}, u32[]{:S(2)}, u32[]{:S(2)}) collective-permute-start(f32[128,256]{0,1:T(8,128)S(1)} %get-tuple-element.54), channel_id=1, source_target_pairs={{1,0},{2,1},{3,2},{4,3},{5,4},{6,5},{7,6},{8,7},{9,8},{10,9},{11,1... | collective-permute-start | bytes 393224 | tf_op jit(solution)/shard_map/ppermute | solution.py:17
  160.6 15.0 %collective-permute-start.11 = (f32[128,256]{0,1:T(8,128)S(1)}, f32[128,256]{0,1:T(8,128)S(1)}, u32[]{:S(2)}, u32[]{:S(2)}) collective-permute-start(f32[128,256]{0,1:T(8,128)S(1)} %get-tuple-element.51), channel_id=1, source_target_pairs={{32,0},{64,32},{96,64},{128,96},{160,128},{192,160},{224,192},{33,... | collective-permute-start | bytes 393224 | tf_op jit(solution)/shard_map/ppermute | solution.py:17
  171.2 4.3 %collective-permute-start.10 = (f32[128,256]{0,1:T(8,128)S(1)}, f32[128,256]{0,1:T(8,128)S(1)}, u32[]{:S(2)}, u32[]{:S(2)}) collective-permute-start(f32[128,256]{0,1:T(8,128)S(1)} %get-tuple-element.52), channel_id=1, source_target_pairs={{0,32},{32,64},{64,96},{96,128},{128,160},{160,192},{192,224},{1,3... | collective-permute-start | bytes 393224 | tf_op jit(solution)/shard_map/ppermute | solution.py:17
  179.4 12.7 %collective-permute-start.12 = (f32[128,256]{0,1:T(8,128)S(1)}, f32[128,256]{0,1:T(8,128)S(1)}, u32[]{:S(2)}, u32[]{:S(2)}) collective-permute-start(f32[128,256]{0,1:T(8,128)S(1)} %get-tuple-element.49), channel_id=1, source_target_pairs={{0,1},{1,2},{2,3},{3,4},{4,5},{5,6},{6,7},{7,8},{8,9},{9,10},{10,1... | collective-permute-start | bytes 393224 | tf_op jit(solution)/shard_map/ppermute | solution.py:17
  184.1 12.7 %collective-permute-start.15 = (f32[128,256]{0,1:T(8,128)S(1)}, f32[128,256]{0,1:T(8,128)S(1)}, u32[]{:S(2)}, u32[]{:S(2)}) collective-permute-start(f32[128,256]{0,1:T(8,128)S(1)} %get-tuple-element.47), channel_id=1, source_target_pairs={{32,0},{64,32},{96,64},{128,96},{160,128},{192,160},{224,192},{33,... | collective-permute-start | bytes 393224 | tf_op jit(solution)/shard_map/ppermute | solution.py:17
  186.1 10.7 %collective-permute-start.14 = (f32[128,256]{0,1:T(8,128)S(1)}, f32[128,256]{0,1:T(8,128)S(1)}, u32[]{:S(2)}, u32[]{:S(2)}) collective-permute-start(f32[128,256]{0,1:T(8,128)S(1)} %get-tuple-element.48), channel_id=1, source_target_pairs={{0,32},{32,64},{64,96},{96,128},{128,160},{160,192},{192,224},{1,3... | collective-permute-start | bytes 393224 | tf_op jit(solution)/shard_map/ppermute | solution.py:17
  190.7 6.0 %collective-permute-start.13 = (f32[128,256]{0,1:T(8,128)S(1)}, f32[128,256]{0,1:T(8,128)S(1)}, u32[]{:S(2)}, u32[]{:S(2)}) collective-permute-start(f32[128,256]{0,1:T(8,128)S(1)} %get-tuple-element.50), channel_id=1, source_target_pairs={{1,0},{2,1},{3,2},{4,3},{5,4},{6,5},{7,6},{8,7},{9,8},{10,9},{11,1... | collective-permute-start | bytes 393224 | tf_op jit(solution)/shard_map/ppermute | solution.py:17
  262.0 7.4 %collective-permute-start.16 = (f32[128,256]{0,1:T(8,128)S(1)}, f32[128,256]{0,1:T(8,128)S(1)}, u32[]{:S(2)}, u32[]{:S(2)}) collective-permute-start(f32[128,256]{0,1:T(8,128)S(1)} %constant_dynamic-slice_fusion), channel_id=1, source_target_pairs={{0,1},{1,2},{2,3},{3,4},{4,5},{5,6},{6,7},{7,8},{8,9},{9,10},{10,1... | collective-permute-start | bytes 393224 | tf_op jit(solution)/shard_map/ppermute | solution.py:17
  269.4 14.1 %collective-permute-start.17 = (f32[128,256]{0,1:T(8,128)S(1)}, f32[128,256]{0,1:T(8,128)S(1)}, u32[]{:S(2)}, u32[]{:S(2)}) collective-permute-start(f32[128,256]{0,1:T(8,128)S(1)} %get-tuple-element.46), channel_id=1, source_target_pairs={{1,0},{2,1},{3,2},{4,3},{5,4},{6,5},{7,6},{8,7},{9,8},{10,9},{11,1... | collective-permute-start | bytes 393224 | tf_op jit(solution)/shard_map/ppermute | solution.py:17
  270.7 14.5 %collective-permute-start.19 = (f32[128,256]{0,1:T(8,128)S(1)}, f32[128,256]{0,1:T(8,128)S(1)}, u32[]{:S(2)}, u32[]{:S(2)}) collective-permute-start(f32[128,256]{0,1:T(8,128)S(1)} %get-tuple-element.43), channel_id=1, source_target_pairs={{32,0},{64,32},{96,64},{128,96},{160,128},{192,160},{224,192},{33,... | collective-permute-start | bytes 393224 | tf_op jit(solution)/shard_map/ppermute | solution.py:17
  289.1 12.8 %collective-permute-start.20 = (f32[128,256]{0,1:T(8,128)S(1)}, f32[128,256]{0,1:T(8,128)S(1)}, u32[]{:S(2)}, u32[]{:S(2)}) collective-permute-start(f32[128,256]{0,1:T(8,128)S(1)} %get-tuple-element.41), channel_id=1, source_target_pairs={{0,1},{1,2},{2,3},{3,4},{4,5},{5,6},{6,7},{7,8},{8,9},{9,10},{10,1... | collective-permute-start | bytes 393224 | tf_op jit(solution)/shard_map/ppermute | solution.py:17
  294.0 12.7 %collective-permute-start.23 = (f32[128,256]{0,1:T(8,128)S(1)}, f32[128,256]{0,1:T(8,128)S(1)}, u32[]{:S(2)}, u32[]{:S(2)}) collective-permute-start(f32[128,256]{0,1:T(8,128)S(1)} %get-tuple-element.39), channel_id=1, source_target_pairs={{32,0},{64,32},{96,64},{128,96},{160,128},{192,160},{224,192},{33,... | collective-permute-start | bytes 393224 | tf_op jit(solution)/shard_map/ppermute | solution.py:17
  295.9 10.7 %collective-permute-start.22 = (f32[128,256]{0,1:T(8,128)S(1)}, f32[128,256]{0,1:T(8,128)S(1)}, u32[]{:S(2)}, u32[]{:S(2)}) collective-permute-start(f32[128,256]{0,1:T(8,128)S(1)} %get-tuple-element.40), channel_id=1, source_target_pairs={{0,32},{32,64},{64,96},{96,128},{128,160},{160,192},{192,224},{1,3... | collective-permute-start | bytes 393224 | tf_op jit(solution)/shard_map/ppermute | solution.py:17
  300.6 6.0 %collective-permute-start.21 = (f32[128,256]{0,1:T(8,128)S(1)}, f32[128,256]{0,1:T(8,128)S(1)}, u32[]{:S(2)}, u32[]{:S(2)}) collective-permute-start(f32[128,256]{0,1:T(8,128)S(1)} %get-tuple-element.42), channel_id=1, source_target_pairs={{1,0},{2,1},{3,2},{4,3},{5,4},{6,5},{7,6},{8,7},{9,8},{10,9},{11,1... | collective-permute-start | bytes 393224 | tf_op jit(solution)/shard_map/ppermute | solution.py:17
  (14 other events, 388.5 us)
where the time goes:
time: 357 us; the launch traced here: 351 us
  blocking collectives  151 us (42%)
  starting transfers between devices  104 us (29%)
  waiting for transfers between devices  43.2 us (12%)
  matrix products  23.3 us (7%)
  other arithmetic  12.9 us (4%)
  local copies, waits for them, and re-layouts  12.8 us (4%)
  between operations  3.99 us (1%)
    psum x12, blocking collectives, one_axis_at_a_time(): x = lax.psum(x, axis)  104 us
    ppermute x24, starting transfers between devices, from_behind(): lax.ppermute(value, axis, [(source, source + steps) for source in range(i...  92.1 us
    all_to_all x2, blocking collectives, copy_for_each(): return lax.all_to_all(copies, axis, split_axis=0, concat_axis=0, tiled=True)  47.1 us
    ppermute x24, waiting for transfers between devices, from_behind(): lax.ppermute(value, axis, [(source, source + steps) for source in range(i...  22.5 us
    all_to_all x1, waiting for transfers between devices, copy_for_each(): return lax.all_to_all(copies, axis, split_axis=0, concat_axis=0, tiled=True)  20.8 us
    all_to_all x1, starting transfers between devices, copy_for_each(): return lax.all_to_all(copies, axis, split_axis=0, concat_axis=0, tiled=True)  11.9 us
    dot_general x3, matrix products, operator(): product = jnp.dot(matrix, inner, precision=lax.Precision.HIGHEST)  11.2 us
    unnamed x35, local copies, waits for them, and re-layouts  8.34 us
  transfers between devices with their start and end apart: 25, of which 9 were waited for; matrix products, arithmetic and copies ran while one was open for 2% of the time, Pallas kernels for 0%

commit v1 on v0

v1 whole, which is shorter than its diff:
```python
import functools

import jax
import jax.numpy as jnp
from jax import lax
from jax.experimental import pallas as pl
from jax.experimental.pallas import tpu as pltpu
from jax.sharding import PartitionSpec as P

BLOCK = 128
NBLOCKS = 8
ORDER = BLOCK * NBLOCKS
FACE_ROWS = 4 * BLOCK
MODES = 32
SUMS = 8
PACK = MODES + SUMS
ITERS = 3
NZ = 8
CHUNK = 64
F32 = jnp.float32
BF16 = jnp.bfloat16


def split(value):
    high = value.astype(BF16)
    return high, (value - high.astype(F32)).astype(BF16)


def mm(left, right):
    return jnp.dot(left, right, preferred_element_type=F32)


def same(left, right):
    gap = left - right
    return 1 - jnp.minimum(gap * gap, 1)


def fold(value):
    rows, width = value.shape
    return jnp.sum(value.reshape(rows // 8, 8, width), axis=0)


def remote(src, dst, send_sem, recv_sem, device):
    return pltpu.make_async_remote_copy(
        src_ref=src, dst_ref=dst, send_sem=send_sem, recv_sem=recv_sem,
        device_id=device, device_id_type=pl.DeviceIdType.MESH,
    )


def kernel(nx, nz, nc, comp, loads, modes, cinv, fb, er, x_out, r_out, m):
    ns = nx * nz
    c = lax.axis_index("cluster")
    s = lax.axis_index("sub")
    xm = lax.div(s, nz)
    zm = lax.rem(s, nz)
    width = m.raw.shape[1]

    def z_at(step):
        return lax.rem(zm + (step + nz), nz)

    def x_at(step):
        return lax.rem(xm + (step + nx), nx)

    def c_at(step):
        return lax.rem(c + (step + nc), nc)

    def z_peer(step):
        return (c, xm * nz + z_at(step))

    def x_peer(step):
        return (c, x_at(step) * nz + zm)

    def c_peer(step):
        return (c_at(step), s)

    beside = (
        (c, lax.rem(s + ns - 1, ns)),
        (c, lax.rem(s + 1, ns)),
        (c_at(-1), s),
        (c_at(1), s),
    )

    get_loads = pltpu.make_async_copy(loads.at[0, 0], m.raw, m.lsem.at[0])
    get_modes = pltpu.make_async_copy(modes.at[0, 0], m.braw, m.lsem.at[1])
    get_cinv = pltpu.make_async_copy(cinv.at[0], m.mraw, m.lsem.at[2])
    get_comp = pltpu.make_async_copy(comp.at[0, 0], m.craw, m.lsem.at[3])
    get_fb = pltpu.make_async_copy(fb.at[c], m.fbs, m.lsem.at[4])
    get_er = pltpu.make_async_copy(er.at[c], m.ers.at[0], m.lsem.at[5])
    get_er_low = pltpu.make_async_copy(er.at[jnp.maximum(c - 1, 0)], m.ers.at[1], m.lsem.at[6])
    for copy in (get_fb, get_er, get_er_low, get_loads, get_modes, get_cinv, get_comp):
        copy.start()

    barrier = pltpu.get_barrier_semaphore()
    greeted = (
        [z_peer(step) for step in range(1, nz)]
        + [x_peer(step) for step in range(1, nx)]
        + [c_peer(step) for step in range(1, nc)]
        + [beside[0], beside[1]]
    )
    for peer in greeted:
        pl.semaphore_signal(barrier, inc=1, device_id=peer, device_id_type=pl.DeviceIdType.MESH)

    for copy in (get_fb, get_er, get_er_low):
        copy.wait()
    faces = [m.fbs[s, f] for f in range(4)]
    rank = jnp.int32(0)
    pick = [[] for _ in range(NBLOCKS)]
    for b in range(NBLOCKS):
        hits = [same(face, b) for face in faces]
        free = 1 - (hits[0] + hits[1] + hits[2] + hits[3])
        hits = hits + [free * same(rank, j) for j in range(4)]
        for p in range(NBLOCKS):
            pick[p].append(hits[p].astype(F32))
        rank = rank + free

    def gathered(p, parts):
        value = pick[p][0] * parts[0]
        for b in range(1, NBLOCKS):
            value = value + pick[p][b] * parts[b]
        return value

    def scattered(b, parts):
        value = pick[0][b] * parts[0]
        for p in range(1, NBLOCKS):
            value = value + pick[p][b] * parts[p]
        return value

    shared = [
        m.ers[0, jnp.maximum(s - 1, 0), 0] * jnp.minimum(s, 1),
        m.ers[0, s, 0] * jnp.minimum(ns - 1 - s, 1),
        m.ers[1, s, 1] * jnp.minimum(c, 1),
        m.ers[0, s, 1] * jnp.minimum(nc - 1 - c, 1),
    ]
    row_at = lax.broadcasted_iota(jnp.int32, (BLOCK, width), 0)
    for f in range(4):
        m.weight[pl.ds(f * BLOCK, BLOCK), :] = 0.5 * jnp.clip(shared[f] - row_at, 0, 1).astype(F32)

    def halved(face, value):
        return m.weight[pl.ds(face * BLOCK, BLOCK), :] * value

    def rows(p):
        return pl.ds(p * BLOCK, BLOCK)

    def loop_rows(first, count, body):
        def step(i, carry):
            body(pl.ds(pl.multiple_of(first + i * CHUNK, CHUNK), CHUNK))
            return carry
        lax.fori_loop(0, count // CHUNK, step, 0)

    def to_halves(source):
        def body(at):
            high, low = split(source[at, :])
            m.vhi[at, :] = high
            m.vlo[at, :] = low
        return body

    get_modes.wait()
    high, low = split(m.braw[...])
    m.bhl[0:MODES, :] = high
    m.bhl[MODES:2 * MODES, :] = low
    get_loads.wait()
    loop_rows(0, ORDER, to_halves(m.raw))

    def coarse(first, count):
        ks = pl.ds(first, count)
        both = mm(m.bhl[:, ks], m.vhi[ks, :])
        return both[:MODES] + both[MODES:] + mm(m.bhl[0:MODES, ks], m.vlo[ks, :])

    pending = []

    def send(src, dst, send_sem, recv_sem, device):
        copy = remote(src, dst, send_sem, recv_sem, device)
        copy.start()
        pending.append(copy)

    far_first = sorted(range(1, nz), key=lambda step: -min(step, nz - step))

    def z_gather_start(k):
        for step in far_first:
            mine = m.zg.at[k, zm]
            send(mine, mine, m.zss.at[k, step], m.zrs.at[k, step], z_peer(step))

    def z_gather_wait(k):
        for step in reversed(far_first):
            slot = m.zg.at[k, z_at(-step)]
            remote(slot, slot, m.zss.at[k, step], m.zrs.at[k, step], z_peer(step)).wait_recv()

    m.zg[0, zm, 0:MODES, :] = coarse(0, ORDER)
    m.zg[0, zm, MODES:PACK, :] = jnp.zeros((SUMS, width), F32)
    pl.semaphore_wait(barrier, len(greeted))
    z_gather_start(0)

    get_cinv.wait()
    span = nz * MODES
    for step in range(1, nx):
        src = m.mraw.at[:, pl.ds(pl.multiple_of(x_at(step) * span, BLOCK), span)]
        send(src, m.mt.at[xm], m.mss.at[step], m.mrs.at[step], x_peer(step))
    m.mt[xm] = m.mraw[:, pl.ds(pl.multiple_of(xm * span, BLOCK), span)]
    modes_at = [m.braw[:, rows(b)] for b in range(NBLOCKS)]
    for p in range(NBLOCKS):
        part = gathered(p, modes_at)
        high, low = split(part)
        m.bhl[0:MODES, rows(p)] = high
        m.bhl[MODES:2 * MODES, rows(p)] = low
        if p < 4:
            m.bfs[p] = part

    def in_blocks(source, into, combine):
        def step(i, carry):
            parts = [source[pl.ds(pl.multiple_of(b * BLOCK + i * 8, 8), 8), :] for b in range(NBLOCKS)]
            for p in range(NBLOCKS):
                into[pl.ds(pl.multiple_of(p * BLOCK + i * 8, 8), 8), :] = combine(p, parts)
            return carry
        lax.fori_loop(0, BLOCK // 8, step, 0)

    in_blocks(m.raw, m.r, gathered)
    for f in range(4):
        send(m.bfs.at[f], m.bfr.at[f ^ 1], m.bss.at[f], m.brs.at[f ^ 1], beside[f])
    for f in range(4):
        remote(m.r.at[rows(f), :], m.rp.at[rows(f ^ 1), :], m.rss.at[f], m.rrs.at[f ^ 1], beside[f]).start()

    def transposed(high, low):
        stacked = jnp.concatenate([high.astype(F32), low.astype(F32), high.astype(F32), jnp.zeros((MODES, BLOCK), F32)], axis=0)
        return stacked.T.astype(BF16)

    for p in range(NBLOCKS):
        m.bt[rows(p), :] = transposed(m.bhl[0:MODES, rows(p)], m.bhl[MODES:2 * MODES, rows(p)])
    m.yk[3 * MODES:, :] = jnp.zeros((MODES, width), BF16)

    get_comp.wait()
    def columns_in_order(i, carry):
        at = pl.ds(pl.multiple_of(i * 16, 16), 16)
        parts = [m.craw[at, rows(b)] for b in range(NBLOCKS)]
        values = [gathered(q, parts) for q in range(NBLOCKS)]
        for q in range(NBLOCKS):
            m.craw[at, rows(q)] = values[q]
        return carry

    def rows_in_order(i, carry):
        for q in range(NBLOCKS):
            parts = [m.craw[pl.ds(pl.multiple_of(b * BLOCK + i * 16, 16), 16), rows(q)] for b in range(NBLOCKS)]
            for p in range(NBLOCKS):
                at = pl.ds(pl.multiple_of(p * BLOCK + i * 16, 16), 16)
                high, low = split(gathered(p, parts))
                m.chi[at, rows(q)] = high
                m.clo[at, rows(q)] = low
        return carry

    lax.fori_loop(0, ORDER // 16, columns_in_order, 0)
    lax.fori_loop(0, BLOCK // 16, rows_in_order, 0)

    for step in range(1, nx):
        slot = m.mt.at[x_at(-step)]
        remote(slot, slot, m.mss.at[step], m.mrs.at[step], x_peer(step)).wait_recv()
    high, low = split(m.mt[...].reshape(nx * MODES, span))
    m.mhl[0:nx * MODES, :] = high
    m.mhl[nx * MODES:, :] = low
    for f in range(4):
        slot = m.bfr.at[f]
        remote(slot, slot, m.bss.at[f], m.brs.at[f], beside[f]).wait_recv()
        m.bpt[rows(f), :] = transposed(*split(m.bfr[f]))

    def stack_y(value):
        high, low = split(value)
        m.yk[0:MODES, :] = high
        m.yk[MODES:2 * MODES, :] = high
        m.yk[2 * MODES:3 * MODES, :] = low

    def solve_coarse(k):
        z_gather_wait(k)
        high, low = split(m.zg[k, :, 0:MODES, :].reshape(nz * MODES, width))
        both = mm(m.mhl[...], high)
        half = nx * MODES
        part = both[:half] + both[half:] + mm(m.mhl[0:half, :], low)
        m.xs[k, :, 0:MODES, :] = part.reshape(nx, MODES, width)
        sums = m.zg[k, 0, MODES:PACK, :]
        for j in range(1, nz):
            sums = sums + m.zg[k, j, MODES:PACK, :]
        for j in range(nx):
            m.xs[k, j, MODES:PACK, :] = sums
        for step in range(1, nx):
            send(m.xs.at[k, x_at(step)], m.xr.at[k, xm], m.xss.at[k, step], m.xrs.at[k, step], x_peer(step))
        m.xr[k, xm] = m.xs[k, xm]
        for step in range(1, nx):
            slot = m.xr.at[k, x_at(-step)]
            remote(slot, slot, m.xss.at[k, step], m.xrs.at[k, step], x_peer(step)).wait_recv()
        total = m.xr[k, 0]
        for j in range(1, nx):
            total = total + m.xr[k, j]
        m.yo[k] = total[:MODES]
        for f in range(4):
            send(m.yo.at[k], m.yp.at[k, f ^ 1], m.yss.at[k, f], m.yrs.at[k, f ^ 1], beside[f])
        stack_y(total[:MODES])
        return total[MODES:]

    def wait_y(k, f):
        slot = m.yp.at[k, f]
        remote(slot, slot, m.yss.at[k, f], m.yrs.at[k, f], beside[f]).wait_recv()

    def product(into, first, count, k_first, k_count, add):
        ks = pl.ds(k_first, k_count)
        size = 256
        def step(i, carry):
            at = pl.ds(pl.multiple_of(first + i * size, size), size)
            value = mm(m.chi[at, ks], m.vhi[ks, :]) + mm(m.chi[at, ks], m.vlo[ks, :]) + mm(m.clo[at, ks], m.vhi[ks, :])
            if add:
                value = value + into[at, :]
            into[at, :] = value
            return carry
        lax.fori_loop(0, count // size, step, 0)

    def coefficients(sums, old):
        rz, curve = sums[0:1], sums[1:2]
        if old is None:
            return rz, None, rz / curve
        ratio = rz / old[0]
        return rz, ratio, rz / (curve - ratio * rz / old[2])

    solve_coarse(0)
    coeff = None
    for k in range(ITERS):
        z = m.z.at[k]
        t = m.t.at[k]
        if k == 0:
            def new_z(at):
                z[at, :] = m.r[at, :] + mm(m.bt[at, :], m.yk[...])
        else:
            w = m.t.at[k - 1]
            z_old = m.z.at[k - 1]
            _, ratio, alpha = coeff

            def new_z(at, w=w, z_old=z_old, ratio=ratio, alpha=alpha, z=z):
                value = w[at, :] + mm(m.bt[at, :], m.yk[...])
                if ratio is not None:
                    value = value + ratio * m.q[at, :]
                m.q[at, :] = value
                z[at, :] = z_old[at, :] - alpha * value
        loop_rows(0, ORDER, new_z)
        loop_rows(FACE_ROWS, ORDER - FACE_ROWS, to_halves(z))
        product(t, 0, ORDER, FACE_ROWS, ORDER - FACE_ROWS, False)
        for f in range(4):
            wait_y(k, f)
            if k == 0:
                slot = m.rp.at[rows(f), :]
                copy = remote(slot, slot, m.rss.at[f], m.rrs.at[f], beside[f])
                copy.wait_recv()
                copy.wait_send()
            stack_y(m.yp[k, f])
            value = mm(m.bpt[rows(f), :], m.yk[...])
            if k == 0:
                value = m.rp[rows(f), :] + value
            else:
                value = m.wp[rows(f), :] + value
                if ratio is not None:
                    value = value + ratio * m.qp[rows(f), :]
                m.qp[rows(f), :] = value
                value = m.zp[rows(f), :] - alpha * value
            m.zp[rows(f), :] = value
            inner = z[rows(f), :] + halved(f, value)
            m.inner[rows(f), :] = inner
            high, low = split(inner)
            m.vhi[rows(f), :] = high
            m.vlo[rows(f), :] = low
        product(t, 0, FACE_ROWS, 0, FACE_ROWS, True)
        m.ts[k] = t[0:FACE_ROWS, :]
        for f in range(4):
            send(m.ts.at[k, rows(f), :], m.tp.at[k, rows(f ^ 1), :], m.tss.at[k, f], m.trs.at[k, f ^ 1], beside[f])
        product(t, FACE_ROWS, ORDER - FACE_ROWS, 0, FACE_ROWS, True)
        if k > 0:
            def update(at, w=w, z_old=z_old, ratio=ratio, alpha=alpha, first=(k == 1)):
                s_new, d_new = w[at, :], z_old[at, :]
                if ratio is not None:
                    s_new = s_new + ratio * m.s[at, :]
                    d_new = d_new + ratio * m.d[at, :]
                m.s[at, :] = s_new
                m.d[at, :] = d_new
                m.x[at, :] = alpha * d_new if first else m.x[at, :] + alpha * d_new
                m.r[at, :] = m.r[at, :] - alpha * s_new
            loop_rows(0, ORDER, update)

        def dots(i, carry, z=z, t=t):
            at = pl.ds(pl.multiple_of(i * CHUNK, CHUNK), CHUNK)
            low_at = pl.ds(pl.multiple_of(FACE_ROWS + i * CHUNK, CHUNK), CHUNK)
            first = carry[0] + fold(m.r[at, :] * z[at, :]) + fold(m.r[low_at, :] * z[low_at, :])
            second = carry[1] + fold(m.inner[at, :] * t[at, :]) + fold(z[low_at, :] * t[low_at, :])
            return first, second
        zero = jnp.zeros((8, width), F32)
        first, second = lax.fori_loop(0, FACE_ROWS // CHUNK, dots, (zero, zero))
        m.cd[k, c, 0:1, :] = jnp.sum(first, axis=0, keepdims=True)
        m.cd[k, c, 1:2, :] = jnp.sum(second, axis=0, keepdims=True)
        m.cd[k, c, 2:8, :] = jnp.zeros((6, width), F32)
        for step in range(1, nc):
            mine = m.cd.at[k, c]
            send(mine, mine, m.css.at[k, step], m.crs.at[k, step], c_peer(step))
        if k + 1 < ITERS:
            loop_rows(FACE_ROWS, ORDER - FACE_ROWS, to_halves(t))
            inside = coarse(FACE_ROWS, ORDER - FACE_ROWS)
        for f in range(4):
            slot = m.tp.at[k, rows(f), :]
            remote(slot, slot, m.tss.at[k, f], m.trs.at[k, f], beside[f]).wait_recv()
            own = m.ts[k, rows(f), :]
            theirs = m.tp[k, rows(f), :]
            value = own + halved(f, theirs)
            t[rows(f), :] = value
            if k + 1 < ITERS:
                m.wp[rows(f), :] = theirs + halved(f, own)
                high, low = split(value)
                m.vhi[rows(f), :] = high
                m.vlo[rows(f), :] = low
        for step in range(1, nc):
            slot = m.cd.at[k, c_at(-step)]
            remote(slot, slot, m.css.at[k, step], m.crs.at[k, step], c_peer(step)).wait_recv()
        sums = m.cd[k, 0]
        for j in range(1, nc):
            sums = sums + m.cd[k, j]
        if k + 1 < ITERS:
            m.zg[k + 1, zm, 0:MODES, :] = inside + coarse(0, FACE_ROWS)
            m.zg[k + 1, zm, MODES:PACK, :] = sums
            z_gather_start(k + 1)
            coeff = coefficients(solve_coarse(k + 1), coeff)

    m.zd[zm] = sums
    for step in far_first:
        mine = m.zd.at[zm]
        send(mine, mine, m.fzs.at[step], m.fzr.at[step], z_peer(step))
    z = m.z.at[ITERS - 1]
    t = m.t.at[ITERS - 1]
    for j, source in enumerate((m.x, z, m.d, m.r, t, m.s)):
        in_blocks(source, m.out.at[j], scattered)
    for step in reversed(far_first):
        slot = m.zd.at[z_at(-step)]
        remote(slot, slot, m.fzs.at[step], m.fzr.at[step], z_peer(step)).wait_recv()
    sums = m.zd[0]
    for j in range(1, nz):
        sums = sums + m.zd[j]
    m.xd[xm] = sums
    for step in range(1, nx):
        mine = m.xd.at[xm]
        send(mine, mine, m.fxs.at[step], m.fxr.at[step], x_peer(step))
    for step in range(1, nx):
        slot = m.xd.at[x_at(-step)]
        remote(slot, slot, m.fxs.at[step], m.fxr.at[step], x_peer(step)).wait_recv()
    sums = m.xd[0]
    for j in range(1, nx):
        sums = sums + m.xd[j]
    _, ratio, alpha = coefficients(sums, coeff)
    def finish(at):
        x_out[0, 0, at, :] = m.out[0, at, :] + alpha * (m.out[1, at, :] + ratio * m.out[2, at, :])
        r_out[0, 0, at, :] = m.out[3, at, :] - alpha * (m.out[4, at, :] + ratio * m.out[5, at, :])
    loop_rows(0, ORDER, finish)
    for copy in pending:
        copy.wait_send()


class Names:
    def __init__(self, names, refs):
        for name, ref in zip(names, refs, strict=True):
            setattr(self, name, ref)


def scratch(nx, nz, nc, width):
    vmem, dma = pltpu.VMEM, pltpu.SemaphoreType.DMA
    span = nz * MODES
    full, face = (ORDER, width), (FACE_ROWS, width)
    return dict(
        raw=vmem(full, F32), braw=vmem((MODES, ORDER), F32), mraw=vmem((MODES, nx * span), F32), craw=vmem((ORDER, ORDER), F32),
        fbs=pltpu.SMEM((nx * nz, 4), jnp.int32), ers=pltpu.SMEM((2, nx * nz, 2), jnp.int32),
        chi=vmem((ORDER, ORDER), BF16), clo=vmem((ORDER, ORDER), BF16), vhi=vmem(full, BF16), vlo=vmem(full, BF16),
        bhl=vmem((2 * MODES, ORDER), BF16), bt=vmem((ORDER, BLOCK), BF16), bpt=vmem((FACE_ROWS, BLOCK), BF16),
        yk=vmem((BLOCK, width), BF16), mt=vmem((nx, MODES, span), F32), mhl=vmem((2 * nx * MODES, span), BF16),
        zg=vmem((ITERS, nz, PACK, width), F32), xs=vmem((ITERS, nx, PACK, width), F32), xr=vmem((ITERS, nx, PACK, width), F32),
        yo=vmem((ITERS, MODES, width), F32), yp=vmem((ITERS, 4, MODES, width), F32),
        ts=vmem((ITERS, *face), F32), tp=vmem((ITERS, *face), F32), cd=vmem((ITERS, nc, SUMS, width), F32),
        zd=vmem((nz, SUMS, width), F32), xd=vmem((nx, SUMS, width), F32),
        bfs=vmem((4, MODES, BLOCK), F32), bfr=vmem((4, MODES, BLOCK), F32), rp=vmem(face, F32),
        z=vmem((ITERS, *full), F32), t=vmem((ITERS, *full), F32), q=vmem(full, F32), s=vmem(full, F32), r=vmem(full, F32),
        d=vmem(full, F32), x=vmem(full, F32), zp=vmem(face, F32), qp=vmem(face, F32), wp=vmem(face, F32), inner=vmem(face, F32), weight=vmem(face, F32), out=vmem((6, *full), F32),
        lsem=dma((8,)), zss=dma((ITERS, nz)), zrs=dma((ITERS, nz)), xss=dma((ITERS, nx)), xrs=dma((ITERS, nx)),
        yss=dma((ITERS, 4)), yrs=dma((ITERS, 4)), tss=dma((ITERS, 4)), trs=dma((ITERS, 4)), css=dma((ITERS, nc)), crs=dma((ITERS, nc)),
        fzs=dma((nz,)), fzr=dma((nz,)), fxs=dma((nx,)), fxr=dma((nx,)), mss=dma((nx,)), mrs=dma((nx,)),
        bss=dma((4,)), brs=dma((4,)), rss=dma((4,)), rrs=dma((4,)),
    )


def shards(nx, nz, nc, compliance, loads, modes, coarse_inverse, face_block, edge_rows):
    width = loads.shape[-1]
    held = scratch(nx, nz, nc, width)

    def body(*refs):
        kernel(nx, nz, nc, *refs[:8], Names(held, refs[8:]))

    anywhere = pl.BlockSpec(memory_space=pl.ANY)
    return pl.pallas_call(
        body,
        out_shape=[jax.ShapeDtypeStruct(loads.shape, F32)] * 2,
        in_specs=[anywhere] * 6,
        out_specs=[pl.BlockSpec(memory_space=pltpu.VMEM)] * 2,
        scratch_shapes=list(held.values()),
        compiler_params=pltpu.CompilerParams(collective_id=0, has_side_effects=True, vmem_limit_bytes=56 * 1024 * 1024),
    )(compliance, loads, modes, coarse_inverse, face_block, edge_rows)


def solution(mesh, nz=NZ):
    nc, ns = mesh.shape["cluster"], mesh.shape["sub"]
    cut = P("cluster", "sub", None, None)
    return jax.shard_map(
        functools.partial(shards, ns // nz, nz, nc), mesh=mesh,
        in_specs=(cut, cut, cut, P("cluster", "sub", None), P(), P()),
        out_specs=(cut, cut), check_vma=False,
    )
```

time: 357 us -> 104 us (0.29); the launches traced: 351 us -> 104 us
  blocking collectives: 151 us -> 0 us
  starting transfers between devices: 104 us -> 0 us
  Pallas kernels: 0 us -> 95.7 us
  waiting for transfers between devices: 43.2 us -> 0 us
  matrix products: 23.3 us -> 0 us
  other arithmetic: 12.9 us -> 0 us
  local copies, waits for them, and re-layouts: 12.8 us -> 7.49 us
    psum x12 -> x0, blocking collectives: 104 us -> none  [one_axis_at_a_time(): x = lax.psum(x, axis)]
    pallas_call x0 -> x1, Pallas kernels: none -> 95.7 us  [shards(): pl.pallas_call(body, out_shape=[jax.ShapeDtypeStruct(loads.shape, F32)] *...]
    ppermute x24 -> x0, starting transfers between devices: 92.1 us -> none  [from_behind(): lax.ppermute(value, axis, [(source, source + steps) for source in range(i...]
    all_to_all x2 -> x0, blocking collectives: 47.1 us -> none  [copy_for_each(): return lax.all_to_all(copies, axis, split_axis=0, concat_axis=0, tiled=True)]
    dot_general x12 -> x0, matrix products: 23.3 us -> none  [the longest x3 11.2 us: operator(): product = jnp.dot(matrix, inner, precision=lax.Precision.HIGHEST)]
    ppermute x24 -> x0, waiting for transfers between devices: 22.5 us -> none  [from_behind(): lax.ppermute(value, axis, [(source, source + steps) for source in range(i...]
    all_to_all x1 -> x0, waiting for transfers between devices: 20.8 us -> none  [copy_for_each(): return lax.all_to_all(copies, axis, split_axis=0, concat_axis=0, tiled=True)]
    all_to_all x1 -> x0, starting transfers between devices: 11.9 us -> none  [copy_for_each(): return lax.all_to_all(copies, axis, split_axis=0, concat_axis=0, tiled=True)]
  transfers between devices with their start and end apart: 25 -> 0, of which waited for: 9 -> 0; matrix products, arithmetic and copies ran while one was open for 2% -> 0% of each run, Pallas kernels for 0% -> 0%
where the time goes in v1:
time: 104 us
  Pallas kernels  95.7 us (92%)
  local copies, waits for them, and re-layouts  7.49 us (7%)
    pallas_call x1, Pallas kernels, shards(): pl.pallas_call(body, out_shape=[jax.ShapeDtypeStruct(loads.shape, F32)] *...  95.7 us
    unnamed x4, local copies, waits for them, and re-layouts  7.49 us

profile of v1, /device:TPU:1, one launch (start us, length us, event | category | flops | bytes accessed | tf_op | source)
XLA Modules:
  0.0 103.8 jit_solution(8629894734298599774)
XLA Ops:
  0.6 1.5 %copy.8.refs_4_ = s32[8,32,4]{2,1,0:T(8,128)} copy(s32[8,32,4]{1,2,0:T(4,128)} %param.10) | data formatting | bytes 8192 | tf_op args[4]
  2.1 1.5 %copy.9.refs_5_ = s32[8,32,2]{2,1,0:T(8,128)} copy(s32[8,32,2]{1,2,0:T(2,128)} %param.11) | data formatting | bytes 4096 | tf_op args[5]
  3.6 95.7 %shard_map.77 = (f32[1,1,1024,256]{3,2,1,0:T(8,128)}, f32[1,1,1024,256]{3,2,1,0:T(8,128)}) custom-call(f32[1,1,1024,1024]{3,2,1,0:T(8,128)} %refs_0_.1, f32[1,1,1024,256]{3,2,1,0:T(8,128)} %refs_1_.1, f32[1,1,32,1024]{3,2,1,0:T(8,128)} %refs_2_.1, f32[1,32,1024]{2,1,0:T(8,128)} %refs_3_.1, s32[8,32,4]{2,1,0:T(8,128)} %copy.8.refs_4_, s32[8,32,2]{2,1,0:T(8,128)} %copy.9.refs_5_), custom_call_target="tpu_custom_call" | custom-call | tf_op jit(solution)/shard_map/pallas_call | solution.py:493
  99.3 2.3 %copy.12 = f32[1,1,1024,256]{3,2,1,0:T(8,128)} copy(f32[1,1,1024,256]{3,2,1,0:T(8,128)} %get-tuple-element.4) | data formatting | bytes 2097152
  101.5 2.3 %copy.13 = f32[1,1,1024,256]{3,2,1,0:T(8,128)} copy(f32[1,1,1024,256]{3,2,1,0:T(8,128)} %get-tuple-element.5) | data formatting | bytes 2097152

commit v2 on v1

--- a/solution.py
+++ b/solution.py
@@ -17,6 +17,7 @@
 ITERS = 3
 NZ = 8
 CHUNK = 64
+WIDE = 256
 F32 = jnp.float32
 BF16 = jnp.bfloat16
 
@@ -47,7 +48,7 @@
     )
 
 
-def kernel(nx, nz, nc, comp, loads, modes, cinv, fb, er, x_out, r_out, m):
+def kernel(nx, nz, nc, comp, loads, modes, cinv, fb, er, x_out, r_out, place_out, m):
     ns = nx * nz
     c = lax.axis_index("cluster")
     s = lax.axis_index("sub")
@@ -102,8 +103,9 @@
 
     for copy in (get_fb, get_er, get_er_low):
         copy.wait()
-    faces = [m.fbs[s, f] for f in range(4)]
+    faces = [m.fbs[f, s] for f in range(4)]
     rank = jnp.int32(0)
+    place = [jnp.int32(0)] * NBLOCKS
     pick = [[] for _ in range(NBLOCKS)]
     for b in range(NBLOCKS):
         hits = [same(face, b) for face in faces]
@@ -111,6 +113,7 @@
         hits = hits + [free * same(rank, j) for j in range(4)]
         for p in range(NBLOCKS):
             pick[p].append(hits[p].astype(F32))
+            place[p] = place[p] + b * hits[p]
         rank = rank + free
 
     def gathered(p, parts):
@@ -119,17 +122,14 @@
             value = value + pick[p][b] * parts[b]
         return value
 
-    def scattered(b, parts):
-        value = pick[0][b] * parts[0]
-        for p in range(1, NBLOCKS):
-            value = value + pick[p][b] * parts[p]
-        return value
+    for p in range(NBLOCKS):
+        place_out[p] = place[p]
 
     shared = [
-        m.ers[0, jnp.maximum(s - 1, 0), 0] * jnp.minimum(s, 1),
-        m.ers[0, s, 0] * jnp.minimum(ns - 1 - s, 1),
-        m.ers[1, s, 1] * jnp.minimum(c, 1),
-        m.ers[0, s, 1] * jnp.minimum(nc - 1 - c, 1),
+        m.ers[0, 0, jnp.maximum(s - 1, 0)] * jnp.minimum(s, 1),
+        m.ers[0, 0, s] * jnp.minimum(ns - 1 - s, 1),
+        m.ers[1, 1, s] * jnp.minimum(c, 1),
+        m.ers[0, 1, s] * jnp.minimum(nc - 1 - c, 1),
     ]
     row_at = lax.broadcasted_iota(jnp.int32, (BLOCK, width), 0)
     for f in range(4):
@@ -175,15 +175,31 @@
 
     far_first = sorted(range(1, nz), key=lambda step: -min(step, nz - step))
 
+    early = 24
+
     def z_gather_start(k):
-        for step in far_first:
+        for step in (2, nz - 2, 1, nz - 1):
             mine = m.zg.at[k, zm]
             send(mine, mine, m.zss.at[k, step], m.zrs.at[k, step], z_peer(step))
 
+    def z_wait(k, step, sem, first=0, count=PACK):
+        slot = m.zg.at[k, z_at(-step), pl.ds(first, count), :]
+        remote(slot, slot, m.zss.at[k, sem], m.zrs.at[k, sem], z_peer(step)).wait_recv()
+
+    def z_gather_forward(k):
+        for sign, first, count, sem in ((1, 0, early, 4), (-1, early, PACK - early, nz)):
+            z_wait(k, 2 * sign, (2 * sign) % nz)
+            slot = m.zg.at[k, z_at(-2 * sign)]
+            step = (3 * sign) % nz
+            send(slot, slot, m.zss.at[k, step], m.zrs.at[k, step], z_peer(sign))
+            slot = m.zg.at[k, z_at(-2 * sign), pl.ds(first, count), :]
+            send(slot, slot, m.zss.at[k, sem], m.zrs.at[k, sem], z_peer(2 * sign))
+
     def z_gather_wait(k):
-        for step in reversed(far_first):
-            slot = m.zg.at[k, z_at(-step)]
-            remote(slot, slot, m.zss.at[k, step], m.zrs.at[k, step], z_peer(step)).wait_recv()
+        for step in (1, -1, 3, -3):
+            z_wait(k, step, step % nz)
+        z_wait(k, 4, 4, 0, early)
+        z_wait(k, 4, nz, early, PACK - early)
 
     m.zg[0, zm, 0:MODES, :] = coarse(0, ORDER)
     m.zg[0, zm, MODES:PACK, :] = jnp.zeros((SUMS, width), F32)
@@ -214,6 +230,7 @@
         lax.fori_loop(0, BLOCK // 8, step, 0)
 
     in_blocks(m.raw, m.r, gathered)
+    z_gather_forward(0)
     for f in range(4):
         send(m.bfs.at[f], m.bfr.at[f ^ 1], m.bss.at[f], m.brs.at[f ^ 1], beside[f])
     for f in range(4):
@@ -225,7 +242,7 @@
 
     for p in range(NBLOCKS):
         m.bt[rows(p), :] = transposed(m.bhl[0:MODES, rows(p)], m.bhl[MODES:2 * MODES, rows(p)])
-    m.yk[3 * MODES:, :] = jnp.zeros((MODES, width), BF16)
+    m.yk[:, 3 * MODES:, :] = jnp.zeros((5, MODES, width), BF16)
 
     get_comp.wait()
     def columns_in_order(i, carry):
@@ -260,11 +277,11 @@
         remote(slot, slot, m.bss.at[f], m.brs.at[f], beside[f]).wait_recv()
         m.bpt[rows(f), :] = transposed(*split(m.bfr[f]))
 
-    def stack_y(value):
+    def stack_y(i, value):
         high, low = split(value)
-        m.yk[0:MODES, :] = high
-        m.yk[MODES:2 * MODES, :] = high
-        m.yk[2 * MODES:3 * MODES, :] = low
+        m.yk[i, 0:MODES, :] = high
+        m.yk[i, MODES:2 * MODES, :] = high
+        m.yk[i, 2 * MODES:3 * MODES, :] = low
 
     def solve_coarse(k):
         z_gather_wait(k)
@@ -290,24 +307,24 @@
         m.yo[k] = total[:MODES]
         for f in range(4):
             send(m.yo.at[k], m.yp.at[k, f ^ 1], m.yss.at[k, f], m.yrs.at[k, f ^ 1], beside[f])
-        stack_y(total[:MODES])
+        stack_y(4, total[:MODES])
         return total[MODES:]
 
     def wait_y(k, f):
         slot = m.yp.at[k, f]
         remote(slot, slot, m.yss.at[k, f], m.yrs.at[k, f], beside[f]).wait_recv()
 
-    def product(into, first, count, k_first, k_count, add):
-        ks = pl.ds(k_first, k_count)
-        size = 256
-        def step(i, carry):
-            at = pl.ds(pl.multiple_of(first + i * size, size), size)
-            value = mm(m.chi[at, ks], m.vhi[ks, :]) + mm(m.chi[at, ks], m.vlo[ks, :]) + mm(m.clo[at, ks], m.vhi[ks, :])
-            if add:
-                value = value + into[at, :]
-            into[at, :] = value
-            return carry
-        lax.fori_loop(0, count // size, step, 0)
+    def product(at, ks):
+        return mm(m.chi[at, ks], m.vhi[ks, :]) + mm(m.chi[at, ks], m.vlo[ks, :]) + mm(m.clo[at, ks], m.vhi[ks, :])
+
+    def keep_halves(at, value):
+        high, low = split(value)
+        m.vhi[at, :] = high
+        m.vlo[at, :] = low
+
+    near, inside = pl.ds(0, FACE_ROWS), pl.ds(FACE_ROWS, ORDER - FACE_ROWS)
+    near_parts = [pl.ds(i, WIDE) for i in range(0, FACE_ROWS, WIDE)]
+    inside_parts = [pl.ds(i, WIDE) for i in range(FACE_ROWS, ORDER, WIDE)]
 
     def coefficients(sums, old):
         rz, curve = sums[0:1], sums[1:2]
@@ -321,32 +338,54 @@
     for k in range(ITERS):
         z = m.z.at[k]
         t = m.t.at[k]
-        if k == 0:
-            def new_z(at):
-                z[at, :] = m.r[at, :] + mm(m.bt[at, :], m.yk[...])
-        else:
+        if k > 0:
             w = m.t.at[k - 1]
             z_old = m.z.at[k - 1]
             _, ratio, alpha = coeff
-
-            def new_z(at, w=w, z_old=z_old, ratio=ratio, alpha=alpha, z=z):
-                value = w[at, :] + mm(m.bt[at, :], m.yk[...])
+        for at in inside_parts + near_parts:
+            value = mm(m.bt[at, :], m.yk[4])
+            if k == 0:
+                value = m.r[at, :] + value
+            else:
+                value = w[at, :] + value
                 if ratio is not None:
                     value = value + ratio * m.q[at, :]
                 m.q[at, :] = value
-                z[at, :] = z_old[at, :] - alpha * value
-        loop_rows(0, ORDER, new_z)
-        loop_rows(FACE_ROWS, ORDER - FACE_ROWS, to_halves(z))
-        product(t, 0, ORDER, FACE_ROWS, ORDER - FACE_ROWS, False)
-        for f in range(4):
+                value = z_old[at, :] - alpha * value
+            z[at, :] = value
+            if at in inside_parts:
+                keep_halves(at, value)
+        for at in near_parts + inside_parts:
+            t[at, :] = product(at, inside)
+        def update(i, total, z=z):
+            at = pl.ds(pl.multiple_of(i * CHUNK, CHUNK), CHUNK)
+            r = m.r[at, :]
+            if k > 0:
+                s_new, d_new = w[at, :], z_old[at, :]
+                if ratio is not None:
+                    s_new = s_new + ratio * m.s[at, :]
+                    d_new = d_new + ratio * m.d[at, :]
+                m.s[at, :] = s_new
+                m.d[at, :] = d_new
+                m.x[at, :] = alpha * d_new if k == 1 else m.x[at, :] + alpha * d_new
+                r = r - alpha * s_new
+                m.r[at, :] = r
+            return total + fold(r * z[at, :])
+        zero = jnp.zeros((8, width), F32)
+        first = lax.fori_loop(0, ORDER // CHUNK, update, zero)
+        m.cd[k, c, 0:1, :] = jnp.sum(first, axis=0, keepdims=True)
+        m.cd[k, c, 2:8, :] = jnp.zeros((6, width), F32)
+        for f in (2, 3, 0, 1):
             wait_y(k, f)
             if k == 0:
                 slot = m.rp.at[rows(f), :]
                 copy = remote(slot, slot, m.rss.at[f], m.rrs.at[f], beside[f])
                 copy.wait_recv()
                 copy.wait_send()
-            stack_y(m.yp[k, f])
-            value = mm(m.bpt[rows(f), :], m.yk[...])
+        for f in range(4):
+            stack_y(f, m.yp[k, f])
+        for f in range(4):
+            value = mm(m.bpt[rows(f), :], m.yk[f])
             if k == 0:
                 value = m.rp[rows(f), :] + value
             else:
@@ -358,55 +397,41 @@
             m.zp[rows(f), :] = value
             inner = z[rows(f), :] + halved(f, value)
             m.inner[rows(f), :] = inner
-            high, low = split(inner)
-            m.vhi[rows(f), :] = high
-            m.vlo[rows(f), :] = low
-        product(t, 0, FACE_ROWS, 0, FACE_ROWS, True)
-        m.ts[k] = t[0:FACE_ROWS, :]
+            keep_halves(rows(f), inner)
+        for at in near_parts:
+            m.ts[k, at, :] = t[at, :] + product(at, near)
         for f in range(4):
             send(m.ts.at[k, rows(f), :], m.tp.at[k, rows(f ^ 1), :], m.tss.at[k, f], m.trs.at[k, f ^ 1], beside[f])
-        product(t, FACE_ROWS, ORDER - FACE_ROWS, 0, FACE_ROWS, True)
-        if k > 0:
-            def update(at, w=w, z_old=z_old, ratio=ratio, alpha=alpha, first=(k == 1)):
-                s_new, d_new = w[at, :], z_old[at, :]
-                if ratio is not None:
-                    s_new = s_new + ratio * m.s[at, :]
-                    d_new = d_new + ratio * m.d[at, :]
-                m.s[at, :] = s_new
-                m.d[at, :] = d_new
-                m.x[at, :] = alpha * d_new if first else m.x[at, :] + alpha * d_new
-                m.r[at, :] = m.r[at, :] - alpha * s_new
-            loop_rows(0, ORDER, update)
-
-        def dots(i, carry, z=z, t=t):
+        for at in inside_parts:
+            value = t[at, :] + product(at, near)
+            t[at, :] = value
+            if k + 1 < ITERS:
+                keep_halves(at, value)
+
+        def dots(i, total, z=z, t=t, k=k):
             at = pl.ds(pl.multiple_of(i * CHUNK, CHUNK), CHUNK)
             low_at = pl.ds(pl.multiple_of(FACE_ROWS + i * CHUNK, CHUNK), CHUNK)
-            first = carry[0] + fold(m.r[at, :] * z[at, :]) + fold(m.r[low_at, :] * z[low_at, :])
-            second = carry[1] + fold(m.inner[at, :] * t[at, :]) + fold(z[low_at, :] * t[low_at, :])
-            return first, second
-        zero = jnp.zeros((8, width), F32)
-        first, second = lax.fori_loop(0, FACE_ROWS // CHUNK, dots, (zero, zero))
-        m.cd[k, c, 0:1, :] = jnp.sum(first, axis=0, keepdims=True)
+            return total + fold(m.inner[at, :] * m.ts[k, at, :]) + fold(z[low_at, :] * t[low_at, :])
+        second = lax.fori_loop(0, FACE_ROWS // CHUNK, dots, zero)
         m.cd[k, c, 1:2, :] = jnp.sum(second, axis=0, keepdims=True)
-        m.cd[k, c, 2:8, :] = jnp.zeros((6, width), F32)
         for step in range(1, nc):
             mine = m.cd.at[k, c]
             send(mine, mine, m.css.at[k, step], m.crs.at[k, step], c_peer(step))
         if k + 1 < ITERS:
-            loop_rows(FACE_ROWS, ORDER - FACE_ROWS, to_halves(t))
-            inside = coarse(FACE_ROWS, ORDER - FACE_ROWS)
+            part = coarse(FACE_ROWS, ORDER - FACE_ROWS)
         for f in range(4):
             slot = m.tp.at[k, rows(f), :]
             remote(slot, slot, m.tss.at[k, f], m.trs.at[k, f], beside[f]).wait_recv()
+        for f in range(4):
             own = m.ts[k, rows(f), :]
             theirs = m.tp[k, rows(f), :]
             value = own + halved(f, theirs)
             t[rows(f), :] = value
             if k + 1 < ITERS:
                 m.wp[rows(f), :] = theirs + halved(f, own)
-                high, low = split(value)
-                m.vhi[rows(f), :] = high
-                m.vlo[rows(f), :] = low
+                keep_halves(rows(f), value)
+        if k + 1 < ITERS:
+            part = part + coarse(0, FACE_ROWS)
         for step in range(1, nc):
             slot = m.cd.at[k, c_at(-step)]
             remote(slot, slot, m.css.at[k, step], m.crs.at[k, step], c_peer(step)).wait_recv()
@@ -414,19 +439,16 @@
         for j in range(1, nc):
             sums = sums + m.cd[k, j]
         if k + 1 < ITERS:
-            m.zg[k + 1, zm, 0:MODES, :] = inside + coarse(0, FACE_ROWS)
+            m.zg[k + 1, zm, 0:MODES, :] = part
             m.zg[k + 1, zm, MODES:PACK, :] = sums
             z_gather_start(k + 1)
+            z_gather_forward(k + 1)
             coeff = coefficients(solve_coarse(k + 1), coeff)
 
     m.zd[zm] = sums
     for step in far_first:
         mine = m.zd.at[zm]
         send(mine, mine, m.fzs.at[step], m.fzr.at[step], z_peer(step))
-    z = m.z.at[ITERS - 1]
-    t = m.t.at[ITERS - 1]
-    for j, source in enumerate((m.x, z, m.d, m.r, t, m.s)):
-        in_blocks(source, m.out.at[j], scattered)
     for step in reversed(far_first):
         slot = m.zd.at[z_at(-step)]
         remote(slot, slot, m.fzs.at[step], m.fzr.at[step], z_peer(step)).wait_recv()
@@ -444,10 +466,22 @@
     for j in range(1, nx):
         sums = sums + m.xd[j]
     _, ratio, alpha = coefficients(sums, coeff)
+    z = m.z.at[ITERS - 1]
+    t = m.t.at[ITERS - 1]
+
     def finish(at):
-        x_out[0, 0, at, :] = m.out[0, at, :] + alpha * (m.out[1, at, :] + ratio * m.out[2, at, :])
-        r_out[0, 0, at, :] = m.out[3, at, :] - alpha * (m.out[4, at, :] + ratio * m.out[5, at, :])
-    loop_rows(0, ORDER, finish)
+        m.out[0, at, :] = m.x[at, :] + alpha * (z[at, :] + ratio * m.d[at, :])
+        m.out[1, at, :] = m.r[at, :] - alpha * (t[at, :] + ratio * m.s[at, :])
+    half = ORDER // 2
+    outs = []
+    for i in range(2):
+        loop_rows(i * half, half, finish)
+        at = pl.ds(i * half, half)
+        for j, into in enumerate((x_out, r_out)):
+            outs.append(pltpu.make_async_copy(m.out.at[j, at, :], into.at[0, 0, at, :], m.lsem.at[2 * i + j]))
+            outs[-1].start()
+    for copy in outs:
+        copy.wait()
     for copy in pending:
         copy.wait_send()
 
@@ -464,40 +498,60 @@
     full, face = (ORDER, width), (FACE_ROWS, width)
     return dict(
         raw=vmem(full, F32), braw=vmem((MODES, ORDER), F32), mraw=vmem((MODES, nx * span), F32), craw=vmem((ORDER, ORDER), F32),
-        fbs=pltpu.SMEM((nx * nz, 4), jnp.int32), ers=pltpu.SMEM((2, nx * nz, 2), jnp.int32),
+        fbs=pltpu.SMEM((4, nx * nz), jnp.int32), ers=pltpu.SMEM((2, 2, nx * nz), jnp.int32),
         chi=vmem((ORDER, ORDER), BF16), clo=vmem((ORDER, ORDER), BF16), vhi=vmem(full, BF16), vlo=vmem(full, BF16),
         bhl=vmem((2 * MODES, ORDER), BF16), bt=vmem((ORDER, BLOCK), BF16), bpt=vmem((FACE_ROWS, BLOCK), BF16),
-        yk=vmem((BLOCK, width), BF16), mt=vmem((nx, MODES, span), F32), mhl=vmem((2 * nx * MODES, span), BF16),
+        yk=vmem((5, BLOCK, width), BF16), mt=vmem((nx, MODES, span), F32), mhl=vmem((2 * nx * MODES, span), BF16),
         zg=vmem((ITERS, nz, PACK, width), F32), xs=vmem((ITERS, nx, PACK, width), F32), xr=vmem((ITERS, nx, PACK, width), F32),
         yo=vmem((ITERS, MODES, width), F32), yp=vmem((ITERS, 4, MODES, width), F32),
         ts=vmem((ITERS, *face), F32), tp=vmem((ITERS, *face), F32), cd=vmem((ITERS, nc, SUMS, width), F32),
         zd=vmem((nz, SUMS, width), F32), xd=vmem((nx, SUMS, width), F32),
         bfs=vmem((4, MODES, BLOCK), F32), bfr=vmem((4, MODES, BLOCK), F32), rp=vmem(face, F32),
         z=vmem((ITERS, *full), F32), t=vmem((ITERS, *full), F32), q=vmem(full, F32), s=vmem(full, F32), r=vmem(full, F32),
-        d=vmem(full, F32), x=vmem(full, F32), zp=vmem(face, F32), qp=vmem(face, F32), wp=vmem(face, F32), inner=vmem(face, F32), weight=vmem(face, F32), out=vmem((6, *full), F32),
-        lsem=dma((8,)), zss=dma((ITERS, nz)), zrs=dma((ITERS, nz)), xss=dma((ITERS, nx)), xrs=dma((ITERS, nx)),
+        d=vmem(full, F32), x=vmem(full, F32), zp=vmem(face, F32), qp=vmem(face, F32), wp=vmem(face, F32), inner=vmem(face, F32), weight=vmem(face, F32), out=vmem((2, *full), F32),
+        lsem=dma((8,)), zss=dma((ITERS, nz + 1)), zrs=dma((ITERS, nz + 1)), xss=dma((ITERS, nx)), xrs=dma((ITERS, nx)),
         yss=dma((ITERS, 4)), yrs=dma((ITERS, 4)), tss=dma((ITERS, 4)), trs=dma((ITERS, 4)), css=dma((ITERS, nc)), crs=dma((ITERS, nc)),
         fzs=dma((nz,)), fzr=dma((nz,)), fxs=dma((nx,)), fxr=dma((nx,)), mss=dma((nx,)), mrs=dma((nx,)),
         bss=dma((4,)), brs=dma((4,)), rss=dma((4,)), rrs=dma((4,)),
     )
 
 
+def back_in_place(place, x, r, x_out, r_out, sems):
+    copies = []
+    for p in range(NBLOCKS):
+        at = pl.ds(pl.multiple_of(place[p] * BLOCK, BLOCK), BLOCK)
+        for j, (source, into) in enumerate(((x, x_out), (r, r_out))):
+            copies.append(pltpu.make_async_copy(source.at[0, 0, pl.ds(p * BLOCK, BLOCK), :], into.at[0, 0, at, :], sems.at[j, p]))
+            copies[-1].start()
+    for copy in copies:
+        copy.wait()
+
+
 def shards(nx, nz, nc, compliance, loads, modes, coarse_inverse, face_block, edge_rows):
     width = loads.shape[-1]
     held = scratch(nx, nz, nc, width)
 
     def body(*refs):
-        kernel(nx, nz, nc, *refs[:8], Names(held, refs[8:]))
+        kernel(nx, nz, nc, *refs[:9], Names(held, refs[9:]))
 
     anywhere = pl.BlockSpec(memory_space=pl.ANY)
-    return pl.pallas_call(
+    small = pl.BlockSpec(memory_space=pltpu.SMEM)
+    shapes = [jax.ShapeDtypeStruct(loads.shape, F32)] * 2
+    x, r, place = pl.pallas_call(
         body,
-        out_shape=[jax.ShapeDtypeStruct(loads.shape, F32)] * 2,
+        out_shape=shapes + [jax.ShapeDtypeStruct((NBLOCKS,), jnp.int32)],
         in_specs=[anywhere] * 6,
-        out_specs=[pl.BlockSpec(memory_space=pltpu.VMEM)] * 2,
+        out_specs=[anywhere, anywhere, small],
         scratch_shapes=list(held.values()),
         compiler_params=pltpu.CompilerParams(collective_id=0, has_side_effects=True, vmem_limit_bytes=56 * 1024 * 1024),
-    )(compliance, loads, modes, coarse_inverse, face_block, edge_rows)
+    )(compliance, loads, modes, coarse_inverse, jnp.transpose(face_block, (0, 2, 1)), jnp.transpose(edge_rows, (0, 2, 1)))
+    return pl.pallas_call(
+        back_in_place,
+        out_shape=shapes,
+        in_specs=[small, anywhere, anywhere],
+        out_specs=[anywhere, anywhere],
+        scratch_shapes=[pltpu.SemaphoreType.DMA((2, NBLOCKS))],
+    )(place, x, r)
 
 
 def solution(mesh, nz=NZ):

time: 104 us -> 159 us (1.53)
  Pallas kernels: 95.7 us -> 157 us
  local copies, waits for them, and re-layouts: 7.49 us -> 0 us
    pallas_call x1 -> x2, Pallas kernels: 95.7 us -> 157 us  [the longest x1 92 us: shards(): pl.pallas_call(body, out_shape=shapes + [jax.ShapeDtypeStruct((NBLOCKS,),...]
    unnamed x4 -> x0, local copies, waits for them, and re-layouts: 7.49 us -> none
where the time goes in v2:
time: 159 us; the launch traced here: 158 us
  Pallas kernels  157 us (99%)
    pallas_call x1, Pallas kernels, shards(): pl.pallas_call(body, out_shape=shapes + [jax.ShapeDtypeStruct((NBLOCKS,),...  92 us
    pallas_call x1, Pallas kernels, shards(): pl.pallas_call(back_in_place, out_shape=shapes, in_specs=[small, anywhere...  65.4 us

profile of v2, /device:TPU:1, one launch (start us, length us, event | category | flops | bytes accessed | tf_op | source)
XLA Modules:
  0.0 158.1 jit_solution(13973123095691807110)
XLA Ops:
  0.6 92.0 %shard_map.77 = (f32[1,1,1024,256]{3,2,1,0:T(8,128)}, f32[1,1,1024,256]{3,2,1,0:T(8,128)}, s32[8]{0:T(128)}) custom-call(f32[1,1,1024,1024]{3,2,1,0:T(8,128)} %refs_0_.1, f32[1,1,1024,256]{3,2,1,0:T(8,128)} %refs_1_.1, f32[1,1,32,1024]{3,2,1,0:T(8,128)} %refs_2_.1, f32[1,32,1024]{2,1,0:T(8,128)} %refs_3_.1, s32[8,4,32]{2,1,0:T(4,128)} %bitcast.2, ...), custom_call_target="tpu_custom_call" | custom-call | tf_op jit(solution)/shard_map/pallas_call | solution.py:540
  92.6 65.4 %shard_map.78 = (f32[1,1,1024,256]{3,2,1,0:T(8,128)}, f32[1,1,1024,256]{3,2,1,0:T(8,128)}) custom-call(s32[8]{0:T(128)} %get-tuple-element.5.place, f32[1,1,1024,256]{3,2,1,0:T(8,128)} %get-tuple-element.6.x, f32[1,1,1024,256]{3,2,1,0:T(8,128)} %get-tuple-element.7.r), custom_call_target="tpu_custom_call" | custom-call | tf_op jit(solution)/shard_map/pallas_call | solution.py:548

commit v3 on v2

--- a/solution.py
+++ b/solution.py
@@ -12,8 +12,8 @@
 ORDER = BLOCK * NBLOCKS
 FACE_ROWS = 4 * BLOCK
 MODES = 32
-SUMS = 8
-PACK = MODES + SUMS
+SUMS = 2
+PACK = MODES + 8
 ITERS = 3
 NZ = 8
 CHUNK = 64
@@ -73,6 +73,9 @@
 
     def c_peer(step):
         return (c_at(step), s)
+
+    def cx_peer(step):
+        return (c_at(step[0]), x_at(step[1]) * nz + zm)
 
     beside = (
         (c, lax.rem(s + ns - 1, ns)),
@@ -92,12 +95,11 @@
         copy.start()
 
     barrier = pltpu.get_barrier_semaphore()
-    greeted = (
-        [z_peer(step) for step in range(1, nz)]
-        + [x_peer(step) for step in range(1, nx)]
-        + [c_peer(step) for step in range(1, nc)]
-        + [beside[0], beside[1]]
+    wide = sorted(
+        ((dc, dx) for dc in range(nc) for dx in range(nx) if dc or dx),
+        key=lambda d: -min(d[0], nc - d[0]) - 2 * min(d[1], nx - d[1]),
     )
+    greeted = [z_peer(step) for step in range(1, nz)] + [cx_peer(d) for d in wide] + [beside[0], beside[1]]
     for peer in greeted:
         pl.semaphore_signal(barrier, inc=1, device_id=peer, device_id_type=pl.DeviceIdType.MESH)
 
@@ -175,19 +177,19 @@
 
     far_first = sorted(range(1, nz), key=lambda step: -min(step, nz - step))
 
-    early = 24
+    early = MODES // 2
 
     def z_gather_start(k):
         for step in (2, nz - 2, 1, nz - 1):
             mine = m.zg.at[k, zm]
             send(mine, mine, m.zss.at[k, step], m.zrs.at[k, step], z_peer(step))
 
-    def z_wait(k, step, sem, first=0, count=PACK):
+    def z_wait(k, step, sem, first=0, count=MODES):
         slot = m.zg.at[k, z_at(-step), pl.ds(first, count), :]
         remote(slot, slot, m.zss.at[k, sem], m.zrs.at[k, sem], z_peer(step)).wait_recv()
 
     def z_gather_forward(k):
-        for sign, first, count, sem in ((1, 0, early, 4), (-1, early, PACK - early, nz)):
+        for sign, first, count, sem in ((1, 0, early, 4), (-1, early, MODES - early, nz)):
             z_wait(k, 2 * sign, (2 * sign) % nz)
             slot = m.zg.at[k, z_at(-2 * sign)]
             step = (3 * sign) % nz
@@ -195,14 +197,28 @@
             slot = m.zg.at[k, z_at(-2 * sign), pl.ds(first, count), :]
             send(slot, slot, m.zss.at[k, sem], m.zrs.at[k, sem], z_peer(2 * sign))
 
+    def z_sums(k, value):
+        m.dz[k, zm] = value
+        for step in far_first:
+            mine = m.dz.at[k, zm]
+            send(mine, mine, m.dzs.at[k, step], m.dzr.at[k, step], z_peer(step))
+
+    def z_sums_total(k):
+        for step in reversed(far_first):
+            slot = m.dz.at[k, z_at(-step)]
+            remote(slot, slot, m.dzs.at[k, step], m.dzr.at[k, step], z_peer(step)).wait_recv()
+        total = m.dz[k, 0]
+        for j in range(1, nz):
+            total = total + m.dz[k, j]
+        return total
+
     def z_gather_wait(k):
         for step in (1, -1, 3, -3):
             z_wait(k, step, step % nz)
         z_wait(k, 4, 4, 0, early)
-        z_wait(k, 4, nz, early, PACK - early)
-
-    m.zg[0, zm, 0:MODES, :] = coarse(0, ORDER)
-    m.zg[0, zm, MODES:PACK, :] = jnp.zeros((SUMS, width), F32)
+        z_wait(k, 4, nz, early, MODES - early)
+
+    m.zg[0, zm] = coarse(0, ORDER)
     pl.semaphore_wait(barrier, len(greeted))
     z_gather_start(0)
 
@@ -212,6 +228,8 @@
         src = m.mraw.at[:, pl.ds(pl.multiple_of(x_at(step) * span, BLOCK), span)]
         send(src, m.mt.at[xm], m.mss.at[step], m.mrs.at[step], x_peer(step))
     m.mt[xm] = m.mraw[:, pl.ds(pl.multiple_of(xm * span, BLOCK), span)]
+    for k in range(ITERS):
+        m.xs[k, :, MODES:PACK, :] = jnp.zeros((nx, PACK - MODES, width), F32)
     modes_at = [m.braw[:, rows(b)] for b in range(NBLOCKS)]
     for p in range(NBLOCKS):
         part = gathered(p, modes_at)
@@ -220,31 +238,15 @@
         m.bhl[MODES:2 * MODES, rows(p)] = low
         if p < 4:
             m.bfs[p] = part
-
-    def in_blocks(source, into, combine):
-        def step(i, carry):
-            parts = [source[pl.ds(pl.multiple_of(b * BLOCK + i * 8, 8), 8), :] for b in range(NBLOCKS)]
-            for p in range(NBLOCKS):
-                into[pl.ds(pl.multiple_of(p * BLOCK + i * 8, 8), 8), :] = combine(p, parts)
-            return carry
-        lax.fori_loop(0, BLOCK // 8, step, 0)
-
-    in_blocks(m.raw, m.r, gathered)
-    z_gather_forward(0)
     for f in range(4):
         send(m.bfs.at[f], m.bfr.at[f ^ 1], m.bss.at[f], m.brs.at[f ^ 1], beside[f])
-    for f in range(4):
-        remote(m.r.at[rows(f), :], m.rp.at[rows(f ^ 1), :], m.rss.at[f], m.rrs.at[f ^ 1], beside[f]).start()
-
-    def transposed(high, low):
-        stacked = jnp.concatenate([high.astype(F32), low.astype(F32), high.astype(F32), jnp.zeros((MODES, BLOCK), F32)], axis=0)
-        return stacked.T.astype(BF16)
-
-    for p in range(NBLOCKS):
-        m.bt[rows(p), :] = transposed(m.bhl[0:MODES, rows(p)], m.bhl[MODES:2 * MODES, rows(p)])
-    m.yk[:, 3 * MODES:, :] = jnp.zeros((5, MODES, width), BF16)
-
-    get_comp.wait()
+
+    def in_blocks(i, carry):
+        parts = [m.raw[pl.ds(pl.multiple_of(b * BLOCK + i * 8, 8), 8), :] for b in range(NBLOCKS)]
+        for p in range(NBLOCKS):
+            m.r[pl.ds(pl.multiple_of(p * BLOCK + i * 8, 8), 8), :] = gathered(p, parts)
+        return carry
+
     def columns_in_order(i, carry):
         at = pl.ds(pl.multiple_of(i * 16, 16), 16)
         parts = [m.craw[at, rows(b)] for b in range(NBLOCKS)]
@@ -263,7 +265,20 @@
                 m.clo[at, rows(q)] = low
         return carry
 
+    lax.fori_loop(0, BLOCK // 8, in_blocks, 0)
+    get_comp.wait()
     lax.fori_loop(0, ORDER // 16, columns_in_order, 0)
+    z_gather_forward(0)
+    for f in range(4):
+        remote(m.r.at[rows(f), :], m.rp.at[rows(f ^ 1), :], m.rss.at[f], m.rrs.at[f ^ 1], beside[f]).start()
+
+    def transposed(high, low):
+        stacked = jnp.concatenate([high.astype(F32), low.astype(F32), high.astype(F32), jnp.zeros((MODES, BLOCK), F32)], axis=0)
+        return stacked.T.astype(BF16)
+
+    for p in range(NBLOCKS):
+        m.bt[rows(p), :] = transposed(m.bhl[0:MODES, rows(p)], m.bhl[MODES:2 * MODES, rows(p)])
+    m.yk[:, 3 * MODES:, :] = jnp.zeros((5, MODES, width), BF16)
     lax.fori_loop(0, BLOCK // 16, rows_in_order, 0)
 
     for step in range(1, nx):
@@ -285,16 +300,15 @@
 
     def solve_coarse(k):
         z_gather_wait(k)
-        high, low = split(m.zg[k, :, 0:MODES, :].reshape(nz * MODES, width))
+        high, low = split(m.zg[k].reshape(nz * MODES, width))
         both = mm(m.mhl[...], high)
         half = nx * MODES
         part = both[:half] + both[half:] + mm(m.mhl[0:half, :], low)
         m.xs[k, :, 0:MODES, :] = part.reshape(nx, MODES, width)
-        sums = m.zg[k, 0, MODES:PACK, :]
-        for j in range(1, nz):
-            sums = sums + m.zg[k, j, MODES:PACK, :]
-        for j in range(nx):
-            m.xs[k, j, MODES:PACK, :] = sums
+        if k > 0:
+            sums = z_sums_total(k)
+            for j in range(nx):
+                m.xs[k, j, MODES:MODES + SUMS, :] = sums
         for step in range(1, nx):
             send(m.xs.at[k, x_at(step)], m.xr.at[k, xm], m.xss.at[k, step], m.xrs.at[k, step], x_peer(step))
         m.xr[k, xm] = m.xs[k, xm]
@@ -308,7 +322,7 @@
         for f in range(4):
             send(m.yo.at[k], m.yp.at[k, f ^ 1], m.yss.at[k, f], m.yrs.at[k, f ^ 1], beside[f])
         stack_y(4, total[:MODES])
-        return total[MODES:]
+        return total[MODES:MODES + SUMS]
 
     def wait_y(k, f):
         slot = m.yp.at[k, f]
@@ -373,8 +387,7 @@
             return total + fold(r * z[at, :])
         zero = jnp.zeros((8, width), F32)
         first = lax.fori_loop(0, ORDER // CHUNK, update, zero)
-        m.cd[k, c, 0:1, :] = jnp.sum(first, axis=0, keepdims=True)
-        m.cd[k, c, 2:8, :] = jnp.zeros((6, width), F32)
+        m.own[k, 0:1, :] = jnp.sum(first, axis=0, keepdims=True)
         for f in (2, 3, 0, 1):
             wait_y(k, f)
             if k == 0:
@@ -398,9 +411,8 @@
             inner = z[rows(f), :] + halved(f, value)
             m.inner[rows(f), :] = inner
             keep_halves(rows(f), inner)
-        for at in near_parts:
-            m.ts[k, at, :] = t[at, :] + product(at, near)
         for f in range(4):
+            m.ts[k, rows(f), :] = t[rows(f), :] + product(rows(f), near)
             send(m.ts.at[k, rows(f), :], m.tp.at[k, rows(f ^ 1), :], m.tss.at[k, f], m.trs.at[k, f ^ 1], beside[f])
         for at in inside_parts:
             value = t[at, :] + product(at, near)
@@ -413,10 +425,17 @@
             low_at = pl.ds(pl.multiple_of(FACE_ROWS + i * CHUNK, CHUNK), CHUNK)
             return total + fold(m.inner[at, :] * m.ts[k, at, :]) + fold(z[low_at, :] * t[low_at, :])
         second = lax.fori_loop(0, FACE_ROWS // CHUNK, dots, zero)
-        m.cd[k, c, 1:2, :] = jnp.sum(second, axis=0, keepdims=True)
-        for step in range(1, nc):
-            mine = m.cd.at[k, c]
-            send(mine, mine, m.css.at[k, step], m.crs.at[k, step], c_peer(step))
+        m.own[k, 1:2, :] = jnp.sum(second, axis=0, keepdims=True)
+        if k + 1 < ITERS:
+            m.cd[k, c] = m.own[k]
+            for step in range(1, nc):
+                mine = m.cd.at[k, c]
+                send(mine, mine, m.css.at[k, step], m.crs.at[k, step], c_peer(step))
+        else:
+            m.fd[c, xm] = m.own[k]
+            for dc, dx in wide:
+                mine = m.fd.at[c, xm]
+                send(mine, mine, m.fss.at[dc, dx], m.frs.at[dc, dx], cx_peer((dc, dx)))
         if k + 1 < ITERS:
             part = coarse(FACE_ROWS, ORDER - FACE_ROWS)
         for f in range(4):
@@ -432,39 +451,29 @@
                 keep_halves(rows(f), value)
         if k + 1 < ITERS:
             part = part + coarse(0, FACE_ROWS)
-        for step in range(1, nc):
-            slot = m.cd.at[k, c_at(-step)]
-            remote(slot, slot, m.css.at[k, step], m.crs.at[k, step], c_peer(step)).wait_recv()
-        sums = m.cd[k, 0]
-        for j in range(1, nc):
-            sums = sums + m.cd[k, j]
         if k + 1 < ITERS:
-            m.zg[k + 1, zm, 0:MODES, :] = part
-            m.zg[k + 1, zm, MODES:PACK, :] = sums
+            m.zg[k + 1, zm] = part
             z_gather_start(k + 1)
+            for step in range(1, nc):
+                slot = m.cd.at[k, c_at(-step)]
+                remote(slot, slot, m.css.at[k, step], m.crs.at[k, step], c_peer(step)).wait_recv()
+            sums = m.cd[k, 0]
+            for j in range(1, nc):
+                sums = sums + m.cd[k, j]
+            z_sums(k + 1, sums)
             z_gather_forward(k + 1)
             coeff = coefficients(solve_coarse(k + 1), coeff)
 
-    m.zd[zm] = sums
-    for step in far_first:
-        mine = m.zd.at[zm]
-        send(mine, mine, m.fzs.at[step], m.fzr.at[step], z_peer(step))
-    for step in reversed(far_first):
-        slot = m.zd.at[z_at(-step)]
-        remote(slot, slot, m.fzs.at[step], m.fzr.at[step], z_peer(step)).wait_recv()
-    sums = m.zd[0]
-    for j in range(1, nz):
-        sums = sums + m.zd[j]
-    m.xd[xm] = sums
-    for step in range(1, nx):
-        mine = m.xd.at[xm]
-        send(mine, mine, m.fxs.at[step], m.fxr.at[step], x_peer(step))
-    for step in range(1, nx):
-        slot = m.xd.at[x_at(-step)]
-        remote(slot, slot, m.fxs.at[step], m.fxr.at[step], x_peer(step)).wait_recv()
-    sums = m.xd[0]
-    for j in range(1, nx):
-        sums = sums + m.xd[j]
+    for dc, dx in reversed(wide):
+        slot = m.fd.at[c_at(-dc), x_at(-dx)]
+        remote(slot, slot, m.fss.at[dc, dx], m.frs.at[dc, dx], cx_peer((dc, dx))).wait_recv()
+    sums = m.fd[0, 0]
+    for i in range(nc):
+        for j in range(nx):
+            if i or j:
+                sums = sums + m.fd[i, j]
+    z_sums(0, sums)
+    sums = z_sums_total(0)
     _, ratio, alpha = coefficients(sums, coeff)
     z = m.z.at[ITERS - 1]
     t = m.t.at[ITERS - 1]
@@ -502,29 +511,39 @@
         chi=vmem((ORDER, ORDER), BF16), clo=vmem((ORDER, ORDER), BF16), vhi=vmem(full, BF16), vlo=vmem(full, BF16),
         bhl=vmem((2 * MODES, ORDER), BF16), bt=vmem((ORDER, BLOCK), BF16), bpt=vmem((FACE_ROWS, BLOCK), BF16),
         yk=vmem((5, BLOCK, width), BF16), mt=vmem((nx, MODES, span), F32), mhl=vmem((2 * nx * MODES, span), BF16),
-        zg=vmem((ITERS, nz, PACK, width), F32), xs=vmem((ITERS, nx, PACK, width), F32), xr=vmem((ITERS, nx, PACK, width), F32),
+        zg=vmem((ITERS, nz, MODES, width), F32), xs=vmem((ITERS, nx, PACK, width), F32), xr=vmem((ITERS, nx, PACK, width), F32),
         yo=vmem((ITERS, MODES, width), F32), yp=vmem((ITERS, 4, MODES, width), F32),
         ts=vmem((ITERS, *face), F32), tp=vmem((ITERS, *face), F32), cd=vmem((ITERS, nc, SUMS, width), F32),
-        zd=vmem((nz, SUMS, width), F32), xd=vmem((nx, SUMS, width), F32),
+        own=vmem((ITERS, SUMS, width), F32), dz=vmem((ITERS, nz, SUMS, width), F32), fd=vmem((nc, nx, SUMS, width), F32),
         bfs=vmem((4, MODES, BLOCK), F32), bfr=vmem((4, MODES, BLOCK), F32), rp=vmem(face, F32),
         z=vmem((ITERS, *full), F32), t=vmem((ITERS, *full), F32), q=vmem(full, F32), s=vmem(full, F32), r=vmem(full, F32),
         d=vmem(full, F32), x=vmem(full, F32), zp=vmem(face, F32), qp=vmem(face, F32), wp=vmem(face, F32), inner=vmem(face, F32), weight=vmem(face, F32), out=vmem((2, *full), F32),
         lsem=dma((8,)), zss=dma((ITERS, nz + 1)), zrs=dma((ITERS, nz + 1)), xss=dma((ITERS, nx)), xrs=dma((ITERS, nx)),
         yss=dma((ITERS, 4)), yrs=dma((ITERS, 4)), tss=dma((ITERS, 4)), trs=dma((ITERS, 4)), css=dma((ITERS, nc)), crs=dma((ITERS, nc)),
-        fzs=dma((nz,)), fzr=dma((nz,)), fxs=dma((nx,)), fxr=dma((nx,)), mss=dma((nx,)), mrs=dma((nx,)),
+        dzs=dma((ITERS, nz)), dzr=dma((ITERS, nz)), fss=dma((nc, nx)), frs=dma((nc, nx)), mss=dma((nx,)), mrs=dma((nx,)),
         bss=dma((4,)), brs=dma((4,)), rss=dma((4,)), rrs=dma((4,)),
     )
 
 
-def back_in_place(place, x, r, x_out, r_out, sems):
-    copies = []
-    for p in range(NBLOCKS):
+def back_in_place(place, x, r, x_out, r_out, held, get, put):
+    pairs = [(p, j) for p in range(NBLOCKS) for j in range(2)]
+    sources, intos = (x, r), (x_out, r_out)
+
+    def load(p, j):
+        at = pl.ds(p * BLOCK, BLOCK)
+        return pltpu.make_async_copy(sources[j].at[0, 0, at, :], held.at[j, at, :], get.at[j, p])
+
+    def store(p, j):
         at = pl.ds(pl.multiple_of(place[p] * BLOCK, BLOCK), BLOCK)
-        for j, (source, into) in enumerate(((x, x_out), (r, r_out))):
-            copies.append(pltpu.make_async_copy(source.at[0, 0, pl.ds(p * BLOCK, BLOCK), :], into.at[0, 0, at, :], sems.at[j, p]))
-            copies[-1].start()
-    for copy in copies:
-        copy.wait()
+        return pltpu.make_async_copy(held.at[j, pl.ds(p * BLOCK, BLOCK), :], intos[j].at[0, 0, at, :], put.at[j, p])
+
+    for p, j in pairs:
+        load(p, j).start()
+    for p, j in pairs:
+        load(p, j).wait()
+        store(p, j).start()
+    for p, j in pairs:
+        store(p, j).wait()
 
 
 def shards(nx, nz, nc, compliance, loads, modes, coarse_inverse, face_block, edge_rows):
@@ -550,7 +569,7 @@
         out_shape=shapes,
         in_specs=[small, anywhere, anywhere],
         out_specs=[anywhere, anywhere],
-        scratch_shapes=[pltpu.SemaphoreType.DMA((2, NBLOCKS))],
+        scratch_shapes=[pltpu.VMEM((2, ORDER, width), F32)] + [pltpu.SemaphoreType.DMA((2, NBLOCKS))] * 2,
     )(place, x, r)
 
 

time: 159 us -> 93.8 us (0.59)
  Pallas kernels: 157 us -> 93 us
    pallas_call x1, Pallas kernels: 65.4 us -> 3.23 us  [shards(): pl.pallas_call(back_in_place, out_shape=shapes, in_specs=[small, anywhere...]
    pallas_call x1, Pallas kernels: 92 us -> 89.8 us  [shards(): pl.pallas_call(body, out_shape=shapes + [jax.ShapeDtypeStruct((NBLOCKS,),...]
where the time goes in v3:
time: 93.8 us; the launch traced here: 93.6 us
  Pallas kernels  93 us (99%)
    pallas_call x1, Pallas kernels, shards(): pl.pallas_call(body, out_shape=shapes + [jax.ShapeDtypeStruct((NBLOCKS,),...  89.8 us
    pallas_call x1, Pallas kernels, shards(): pl.pallas_call(back_in_place, out_shape=shapes, in_specs=[small, anywhere...  3.23 us

profile of v3, /device:TPU:1, one launch (start us, length us, event | category | flops | bytes accessed | tf_op | source)
XLA Modules:
  0.0 93.6 jit_solution(17735542143305480353)
XLA Ops:
  0.6 89.8 %shard_map.77 = (f32[1,1,1024,256]{3,2,1,0:T(8,128)}, f32[1,1,1024,256]{3,2,1,0:T(8,128)}, s32[8]{0:T(128)}) custom-call(f32[1,1,1024,1024]{3,2,1,0:T(8,128)} %refs_0_.1, f32[1,1,1024,256]{3,2,1,0:T(8,128)} %refs_1_.1, f32[1,1,32,1024]{3,2,1,0:T(8,128)} %refs_2_.1, f32[1,32,1024]{2,1,0:T(8,128)} %refs_3_.1, s32[8,4,32]{2,1,0:T(4,128)} %bitcast.2, ...), custom_call_target="tpu_custom_call" | custom-call | tf_op jit(solution)/shard_map/pallas_call | solution.py:559
  90.4 3.2 %shard_map.78 = (f32[1,1,1024,256]{3,2,1,0:T(8,128)}, f32[1,1,1024,256]{3,2,1,0:T(8,128)}) custom-call(s32[8]{0:T(128)} %get-tuple-element.5.place, f32[1,1,1024,256]{3,2,1,0:T(8,128)} %get-tuple-element.6.x, f32[1,1,1024,256]{3,2,1,0:T(8,128)} %get-tuple-element.7.r), custom_call_target="tpu_custom_call" | custom-call | tf_op jit(solution)/shard_map/pallas_call | solution.py:567

commit v4 on v3

--- a/solution.py
+++ b/solution.py
@@ -290,13 +290,31 @@
     for f in range(4):
         slot = m.bfr.at[f]
         remote(slot, slot, m.bss.at[f], m.brs.at[f], beside[f]).wait_recv()
-        m.bpt[rows(f), :] = transposed(*split(m.bfr[f]))
+        high, low = split(m.bfr[f])
+        m.bpt[rows(f), :] = transposed(high, low)
+        m.bph[f, 0:MODES, :] = high
+        m.bph[f, MODES:2 * MODES, :] = low
 
     def stack_y(i, value):
         high, low = split(value)
         m.yk[i, 0:MODES, :] = high
         m.yk[i, MODES:2 * MODES, :] = high
         m.yk[i, 2 * MODES:3 * MODES, :] = low
+
+    def send_faces(k):
+        for f in range(4):
+            send(m.ts.at[k, rows(f), :], m.tp.at[k, rows(f ^ 1), :], m.tss.at[k, f], m.trs.at[k, f ^ 1], beside[f])
+
+    def image_on_faces(k):
+        for f in range(4):
+            slot = m.tp.at[k, rows(f), :]
+            remote(slot, slot, m.tss.at[k, f], m.trs.at[k, f], beside[f]).wait_recv()
+        for f in range(4):
+            own = m.ts[k, rows(f), :]
+            theirs = m.tp[k, rows(f), :]
+            m.t[k, rows(f), :] = own + halved(f, theirs)
+            if k + 1 < ITERS:
+                m.wp[rows(f), :] = theirs + halved(f, own)
 
     def solve_coarse(k):
         z_gather_wait(k)
@@ -312,6 +330,8 @@
         for step in range(1, nx):
             send(m.xs.at[k, x_at(step)], m.xr.at[k, xm], m.xss.at[k, step], m.xrs.at[k, step], x_peer(step))
         m.xr[k, xm] = m.xs[k, xm]
+        if k > 0:
+            send_faces(k - 1)
         for step in range(1, nx):
             slot = m.xr.at[k, x_at(-step)]
             remote(slot, slot, m.xss.at[k, step], m.xrs.at[k, step], x_peer(step)).wait_recv()
@@ -356,7 +376,7 @@
             w = m.t.at[k - 1]
             z_old = m.z.at[k - 1]
             _, ratio, alpha = coeff
-        for at in inside_parts + near_parts:
+        def new_z(at):
             value = mm(m.bt[at, :], m.yk[4])
             if k == 0:
                 value = m.r[at, :] + value
@@ -367,10 +387,15 @@
                 m.q[at, :] = value
                 value = z_old[at, :] - alpha * value
             z[at, :] = value
-            if at in inside_parts:
-                keep_halves(at, value)
+            return value
+        for at in inside_parts:
+            keep_halves(at, new_z(at))
         for at in near_parts + inside_parts:
             t[at, :] = product(at, inside)
+        if k > 0:
+            image_on_faces(k - 1)
+        for at in near_parts:
+            new_z(at)
         def update(i, total, z=z):
             at = pl.ds(pl.multiple_of(i * CHUNK, CHUNK), CHUNK)
             r = m.r[at, :]
@@ -413,17 +438,18 @@
             keep_halves(rows(f), inner)
         for f in range(4):
             m.ts[k, rows(f), :] = t[rows(f), :] + product(rows(f), near)
-            send(m.ts.at[k, rows(f), :], m.tp.at[k, rows(f ^ 1), :], m.tss.at[k, f], m.trs.at[k, f ^ 1], beside[f])
-        for at in inside_parts:
-            value = t[at, :] + product(at, near)
-            t[at, :] = value
-            if k + 1 < ITERS:
-                keep_halves(at, value)
-
+        if k + 1 < ITERS:
+            for f in range(4):
+                high, low = split(halved(f, m.ts[k, rows(f), :]))
+                both = mm(m.bph[f], high)
+                m.hs[k, f] = both[:MODES] + both[MODES:] + mm(m.bph[f, 0:MODES, :], low)
+                send(m.hs.at[k, f], m.hr.at[k, f ^ 1], m.hss.at[k, f], m.hrs.at[k, f ^ 1], beside[f])
+        else:
+            send_faces(k)
         def dots(i, total, z=z, t=t, k=k):
             at = pl.ds(pl.multiple_of(i * CHUNK, CHUNK), CHUNK)
             low_at = pl.ds(pl.multiple_of(FACE_ROWS + i * CHUNK, CHUNK), CHUNK)
-            return total + fold(m.inner[at, :] * m.ts[k, at, :]) + fold(z[low_at, :] * t[low_at, :])
+            return total + fold(m.inner[at, :] * (m.ts[k, at, :] + t[at, :])) + fold(z[low_at, :] * t[low_at, :])
         second = lax.fori_loop(0, FACE_ROWS // CHUNK, dots, zero)
         m.own[k, 1:2, :] = jnp.sum(second, axis=0, keepdims=True)
         if k + 1 < ITERS:
@@ -436,22 +462,20 @@
             for dc, dx in wide:
                 mine = m.fd.at[c, xm]
                 send(mine, mine, m.fss.at[dc, dx], m.frs.at[dc, dx], cx_peer((dc, dx)))
+        for at in inside_parts:
+            value = t[at, :] + product(at, near)
+            t[at, :] = value
+            if k + 1 < ITERS:
+                keep_halves(at, value)
+
         if k + 1 < ITERS:
-            part = coarse(FACE_ROWS, ORDER - FACE_ROWS)
-        for f in range(4):
-            slot = m.tp.at[k, rows(f), :]
-            remote(slot, slot, m.tss.at[k, f], m.trs.at[k, f], beside[f]).wait_recv()
-        for f in range(4):
-            own = m.ts[k, rows(f), :]
-            theirs = m.tp[k, rows(f), :]
-            value = own + halved(f, theirs)
-            t[rows(f), :] = value
-            if k + 1 < ITERS:
-                m.wp[rows(f), :] = theirs + halved(f, own)
-                keep_halves(rows(f), value)
-        if k + 1 < ITERS:
-            part = part + coarse(0, FACE_ROWS)
-        if k + 1 < ITERS:
+            for at in near_parts:
+                keep_halves(at, m.ts[k, at, :])
+            part = coarse(0, ORDER)
+            for f in range(4):
+                slot = m.hr.at[k, f]
+                remote(slot, slot, m.hss.at[k, f], m.hrs.at[k, f], beside[f]).wait_recv()
+                part = part + m.hr[k, f]
             m.zg[k + 1, zm] = part
             z_gather_start(k + 1)
             for step in range(1, nc):
@@ -464,6 +488,7 @@
             z_gather_forward(k + 1)
             coeff = coefficients(solve_coarse(k + 1), coeff)
 
+    image_on_faces(ITERS - 1)
     for dc, dx in reversed(wide):
         slot = m.fd.at[c_at(-dc), x_at(-dx)]
         remote(slot, slot, m.fss.at[dc, dx], m.frs.at[dc, dx], cx_peer((dc, dx))).wait_recv()
@@ -509,7 +534,8 @@
         raw=vmem(full, F32), braw=vmem((MODES, ORDER), F32), mraw=vmem((MODES, nx * span), F32), craw=vmem((ORDER, ORDER), F32),
         fbs=pltpu.SMEM((4, nx * nz), jnp.int32), ers=pltpu.SMEM((2, 2, nx * nz), jnp.int32),
         chi=vmem((ORDER, ORDER), BF16), clo=vmem((ORDER, ORDER), BF16), vhi=vmem(full, BF16), vlo=vmem(full, BF16),
-        bhl=vmem((2 * MODES, ORDER), BF16), bt=vmem((ORDER, BLOCK), BF16), bpt=vmem((FACE_ROWS, BLOCK), BF16),
+        bhl=vmem((2 * MODES, ORDER), BF16), bt=vmem((ORDER, BLOCK), BF16), bpt=vmem((FACE_ROWS, BLOCK), BF16), bph=vmem((4, 2 * MODES, BLOCK), BF16),
+        hs=vmem((ITERS, 4, MODES, width), F32), hr=vmem((ITERS, 4, MODES, width), F32), hss=dma((ITERS, 4)), hrs=dma((ITERS, 4)),
         yk=vmem((5, BLOCK, width), BF16), mt=vmem((nx, MODES, span), F32), mhl=vmem((2 * nx * MODES, span), BF16),
         zg=vmem((ITERS, nz, MODES, width), F32), xs=vmem((ITERS, nx, PACK, width), F32), xr=vmem((ITERS, nx, PACK, width), F32),
         yo=vmem((ITERS, MODES, width), F32), yp=vmem((ITERS, 4, MODES, width), F32),
@@ -525,7 +551,7 @@
     )
 
 
-def back_in_place(place, x, r, x_out, r_out, held, get, put):
+def back_in_place(place_in, x, r, x_out, r_out, held, place, get, put, place_sem):
     pairs = [(p, j) for p in range(NBLOCKS) for j in range(2)]
     sources, intos = (x, r), (x_out, r_out)
 
@@ -537,8 +563,11 @@
         at = pl.ds(pl.multiple_of(place[p] * BLOCK, BLOCK), BLOCK)
         return pltpu.make_async_copy(held.at[j, pl.ds(p * BLOCK, BLOCK), :], intos[j].at[0, 0, at, :], put.at[j, p])
 
+    get_place = pltpu.make_async_copy(place_in, place, place_sem)
+    get_place.start()
     for p, j in pairs:
         load(p, j).start()
+    get_place.wait()
     for p, j in pairs:
         load(p, j).wait()
         store(p, j).start()
@@ -567,9 +596,12 @@
     return pl.pallas_call(
         back_in_place,
         out_shape=shapes,
-        in_specs=[small, anywhere, anywhere],
+        in_specs=[anywhere] * 3,
         out_specs=[anywhere, anywhere],
-        scratch_shapes=[pltpu.VMEM((2, ORDER, width), F32)] + [pltpu.SemaphoreType.DMA((2, NBLOCKS))] * 2,
+        scratch_shapes=[
+            pltpu.VMEM((2, ORDER, width), F32), pltpu.SMEM((NBLOCKS,), jnp.int32),
+            pltpu.SemaphoreType.DMA((2, NBLOCKS)), pltpu.SemaphoreType.DMA((2, NBLOCKS)), pltpu.SemaphoreType.DMA,
+        ],
     )(place, x, r)
 
 

time: 93.8 us -> 92.3 us (0.984)
  Pallas kernels: 93 us -> 91.3 us
    pallas_call x1, Pallas kernels: 89.8 us -> 88.7 us  [shards(): pl.pallas_call(body, out_shape=shapes + [jax.ShapeDtypeStruct((NBLOCKS,),...]
where the time goes in v4:
time: 92.3 us; the launch traced here: 92 us
  Pallas kernels  91.3 us (99%)
    pallas_call x1, Pallas kernels, shards(): pl.pallas_call(body, out_shape=shapes + [jax.ShapeDtypeStruct((NBLOCKS,),...  88.7 us
    pallas_call x1, Pallas kernels, shards(): pl.pallas_call(back_in_place, out_shape=shapes, in_specs=[anywhere] * 3,...  2.58 us

profile of v4, /device:TPU:1, one launch (start us, length us, event | category | flops | bytes accessed | tf_op | source)
XLA Modules:
  0.0 92.0 jit_solution(16250883267689854367)
XLA Ops:
  0.6 88.7 %shard_map.77 = (f32[1,1,1024,256]{3,2,1,0:T(8,128)}, f32[1,1,1024,256]{3,2,1,0:T(8,128)}, s32[8]{0:T(128)}) custom-call(f32[1,1,1024,1024]{3,2,1,0:T(8,128)} %refs_0_.1, f32[1,1,1024,256]{3,2,1,0:T(8,128)} %refs_1_.1, f32[1,1,32,1024]{3,2,1,0:T(8,128)} %refs_2_.1, f32[1,32,1024]{2,1,0:T(8,128)} %refs_3_.1, s32[8,4,32]{2,1,0:T(4,128)} %bitcast.2, ...), custom_call_target="tpu_custom_call" | custom-call | tf_op jit(solution)/shard_map/pallas_call | solution.py:588
  89.4 2.6 %shard_map.78 = (f32[1,1,1024,256]{3,2,1,0:T(8,128)}, f32[1,1,1024,256]{3,2,1,0:T(8,128)}) custom-call(s32[8]{0:T(128)} %get-tuple-element.5.place_in, f32[1,1,1024,256]{3,2,1,0:T(8,128)} %get-tuple-element.6.x, f32[1,1,1024,256]{3,2,1,0:T(8,128)} %get-tuple-element.7.r), custom_call_target="tpu_custom_call" | custom-call | tf_op jit(solution)/shard_map/pallas_call | solution.py:596

commit v5 on v4

--- a/solution.py
+++ b/solution.py
@@ -302,7 +302,7 @@
         m.yk[i, 2 * MODES:3 * MODES, :] = low
 
     def send_faces(k):
-        for f in range(4):
+        for f in (2, 3, 0, 1):
             send(m.ts.at[k, rows(f), :], m.tp.at[k, rows(f ^ 1), :], m.tss.at[k, f], m.trs.at[k, f ^ 1], beside[f])
 
     def image_on_faces(k):
@@ -330,8 +330,6 @@
         for step in range(1, nx):
             send(m.xs.at[k, x_at(step)], m.xr.at[k, xm], m.xss.at[k, step], m.xrs.at[k, step], x_peer(step))
         m.xr[k, xm] = m.xs[k, xm]
-        if k > 0:
-            send_faces(k - 1)
         for step in range(1, nx):
             slot = m.xr.at[k, x_at(-step)]
             remote(slot, slot, m.xss.at[k, step], m.xrs.at[k, step], x_peer(step)).wait_recv()
@@ -444,6 +442,7 @@
                 both = mm(m.bph[f], high)
                 m.hs[k, f] = both[:MODES] + both[MODES:] + mm(m.bph[f, 0:MODES, :], low)
                 send(m.hs.at[k, f], m.hr.at[k, f ^ 1], m.hss.at[k, f], m.hrs.at[k, f ^ 1], beside[f])
+            send_faces(k)
         else:
             send_faces(k)
         def dots(i, total, z=z, t=t, k=k):

time: 92.3 us -> 89.9 us (0.974)
  Pallas kernels: 91.3 us -> 89.1 us
    pallas_call x1, Pallas kernels: 88.7 us -> 86.6 us  [shards(): pl.pallas_call(body, out_shape=shapes + [jax.ShapeDtypeStruct((NBLOCKS,),...]
where the time goes in v5:
time: 89.9 us; the launch traced here: 89.8 us
  Pallas kernels  89.1 us (99%)
    pallas_call x1, Pallas kernels, shards(): pl.pallas_call(body, out_shape=shapes + [jax.ShapeDtypeStruct((NBLOCKS,),...  86.6 us
    pallas_call x1, Pallas kernels, shards(): pl.pallas_call(back_in_place, out_shape=shapes, in_specs=[anywhere] * 3,...  2.58 us

profile of v5, /device:TPU:1, one launch (start us, length us, event | category | flops | bytes accessed | tf_op | source)
XLA Modules:
  0.0 89.8 jit_solution(13861434262359302645)
XLA Ops:
  0.6 86.6 %shard_map.77 = (f32[1,1,1024,256]{3,2,1,0:T(8,128)}, f32[1,1,1024,256]{3,2,1,0:T(8,128)}, s32[8]{0:T(128)}) custom-call(f32[1,1,1024,1024]{3,2,1,0:T(8,128)} %refs_0_.1, f32[1,1,1024,256]{3,2,1,0:T(8,128)} %refs_1_.1, f32[1,1,32,1024]{3,2,1,0:T(8,128)} %refs_2_.1, f32[1,32,1024]{2,1,0:T(8,128)} %refs_3_.1, s32[8,4,32]{2,1,0:T(4,128)} %bitcast.2, ...), custom_call_target="tpu_custom_call" | custom-call | tf_op jit(solution)/shard_map/pallas_call | solution.py:587
  87.2 2.6 %shard_map.78 = (f32[1,1,1024,256]{3,2,1,0:T(8,128)}, f32[1,1,1024,256]{3,2,1,0:T(8,128)}) custom-call(s32[8]{0:T(128)} %get-tuple-element.5.place_in, f32[1,1,1024,256]{3,2,1,0:T(8,128)} %get-tuple-element.6.x, f32[1,1,1024,256]{3,2,1,0:T(8,128)} %get-tuple-element.7.r), custom_call_target="tpu_custom_call" | custom-call | tf_op jit(solution)/shard_map/pallas_call | solution.py:595

commit v6 on v5

--- a/solution.py
+++ b/solution.py
@@ -435,13 +435,14 @@
             m.inner[rows(f), :] = inner
             keep_halves(rows(f), inner)
         for f in range(4):
-            m.ts[k, rows(f), :] = t[rows(f), :] + product(rows(f), near)
-        if k + 1 < ITERS:
-            for f in range(4):
-                high, low = split(halved(f, m.ts[k, rows(f), :]))
+            value = t[rows(f), :] + product(rows(f), near)
+            m.ts[k, rows(f), :] = value
+            if k + 1 < ITERS:
+                high, low = split(halved(f, value))
                 both = mm(m.bph[f], high)
                 m.hs[k, f] = both[:MODES] + both[MODES:] + mm(m.bph[f, 0:MODES, :], low)
                 send(m.hs.at[k, f], m.hr.at[k, f ^ 1], m.hss.at[k, f], m.hrs.at[k, f ^ 1], beside[f])
+        if k + 1 < ITERS:
             send_faces(k)
         else:
             send_faces(k)

time: 89.9 us -> 89.9 us (level)
  no operation moved by 1% of the time
where the time goes in v6:
time: 89.9 us; the launch traced here: 89.7 us
  Pallas kernels  89 us (99%)
    pallas_call x1, Pallas kernels, shards(): pl.pallas_call(body, out_shape=shapes + [jax.ShapeDtypeStruct((NBLOCKS,),...  86.5 us
    pallas_call x1, Pallas kernels, shards(): pl.pallas_call(back_in_place, out_shape=shapes, in_specs=[anywhere] * 3,...  2.58 us

profile of v6, /device:TPU:1, one launch (start us, length us, event | category | flops | bytes accessed | tf_op | source)
XLA Modules:
  0.0 89.7 jit_solution(14581052852244006644)
XLA Ops:
  0.6 86.5 %shard_map.77 = (f32[1,1,1024,256]{3,2,1,0:T(8,128)}, f32[1,1,1024,256]{3,2,1,0:T(8,128)}, s32[8]{0:T(128)}) custom-call(f32[1,1,1024,1024]{3,2,1,0:T(8,128)} %refs_0_.1, f32[1,1,1024,256]{3,2,1,0:T(8,128)} %refs_1_.1, f32[1,1,32,1024]{3,2,1,0:T(8,128)} %refs_2_.1, f32[1,32,1024]{2,1,0:T(8,128)} %refs_3_.1, s32[8,4,32]{2,1,0:T(4,128)} %bitcast.2, ...), custom_call_target="tpu_custom_call" | custom-call | tf_op jit(solution)/shard_map/pallas_call | solution.py:588
  87.1 2.6 %shard_map.78 = (f32[1,1,1024,256]{3,2,1,0:T(8,128)}, f32[1,1,1024,256]{3,2,1,0:T(8,128)}) custom-call(s32[8]{0:T(128)} %get-tuple-element.5.place_in, f32[1,1,1024,256]{3,2,1,0:T(8,128)} %get-tuple-element.6.x, f32[1,1,1024,256]{3,2,1,0:T(8,128)} %get-tuple-element.7.r), custom_call_target="tpu_custom_call" | custom-call | tf_op jit(solution)/shard_map/pallas_call | solution.py:596
